TPU v7x, 32 devices: a whole 2x2x4 slice. The times are simulated.
32 devices in a mesh: rows: 4 (over y, x), tm: 8 (over z, core).
Axes of the slice: x: 2, y: 2, z: 4, core: 2. Of those that a mesh axis runs over, the one named last changes fastest.
Arguments:
- frames: bfloat16 [4, 4, 1024, 512], P(None, 'rows', 'tm'), may hold values from -6 to 6
- segment_ids: int32 [4, 4, 1024], P(None, 'rows', 'tm'), may hold values from 0 to 16, as said below
- norm_gains: float32 [2, 5, 512], replicated, may hold values from 0.5 to 1.5
- feed_in: bfloat16 [2, 2, 512, 2048], replicated, may hold values from -0.25 to 0.25
- feed_out: bfloat16 [2, 2, 2048, 512], replicated, may hold values from -0.125 to 0.125
- attend_in: bfloat16 [2, 512, 1536], replicated, may hold values from -0.25 to 0.25
- attend_out: bfloat16 [2, 512, 512], replicated, may hold values from -1.5 to 1.5
- point_in: bfloat16 [2, 512, 1024], replicated, may hold values from -0.25 to 0.25
- depthwise: float32 [2, 9, 512], replicated, may hold values from -2 to 2
- stat_mean: float32 [2, 512], replicated, may hold values from -1.75 to 1.75
- stat_var: float32 [2, 512], replicated, may hold values from 0.2 to 2
- batch_scale: float32 [2, 512], replicated, may hold values from 0.5 to 1.5
- batch_shift: float32 [2, 512], replicated, may hold values from -1.75 to 1.75
- point_out: bfloat16 [2, 512, 512], replicated, may hold values from -0.25 to 0.25
- cotangent: bfloat16 [4, 4, 1024, 512], P(None, 'rows', 'tm'), may hold values from -6 to 6
Outputs:
- activations: bfloat16 [4, 4, 1024, 512], P(None, 'rows', 'tm')
- frames_grad: bfloat16 [4, 4, 1024, 512], P(None, 'rows', 'tm')
- gains_grad: float32 [2, 5, 512], P(None, None, 'tm')
- feed_in_grad: float32 [2, 2, 512, 2048], P(None, None, None, 'tm')
- feed_out_grad: float32 [2, 2, 2048, 512], P(None, None, None, 'tm')
- attend_in_grad: float32 [2, 512, 1536], P(None, None, 'tm')
- attend_out_grad: float32 [2, 512, 512], P(None, None, 'tm')
- point_in_grad: float32 [2, 512, 1024], P(None, None, 'tm')
- depthwise_grad: float32 [2, 9, 512], P(None, None, 'tm')
- scale_grad: float32 [2, 512], P(None, 'tm')
- shift_grad: float32 [2, 512], P(None, 'tm')
- point_out_grad: float32 [2, 512, 512], P(None, None, 'tm')
Inputs may be any that keep to these rules, and one draw needn't show every extreme that they name: `segment_ids`: along each row the ids never fall and rise by one at a time; every utterance is shorter than 128 frames and lies within two adjacent blocks of 128 frames (frames j * 128 to (j + 2) * 128 - 1 for some j); every boundary between two blocks is crossed by an utterance.
All inputs are finite; a program needn't handle non-finite values.
Results may differ from a plain program's by a relative error of at most 0.023.
Values may be sent and summed in bfloat16 or wider, within the bound.
No kernel may reach another device: no remote copies, remote signals or barrier semaphores. Data moves between devices by JAX's collectives and lax.ppermute only.
A program may use at most 384 MiB of HBM per device.

v0:
```python
import jax
import jax.numpy as jnp
from jax import lax
from jax.sharding import PartitionSpec as P

HD = 64
KERNEL = 9
HALO = 4


EPSILON = 1e-05
MASKED = -1e30


def extended_2(array, sides, width):
    for axis, dim in sides:
        size, length = (lax.axis_size(axis), array.shape[dim])
        up = [(i, (i + 1) % size) for i in range(size - 1)]
        down = [(j, i) for i, j in up]
        last = lax.slice_in_dim(array, length - width, length, axis=dim)
        leading = lax.slice_in_dim(array, 0, width, axis=dim)
        before = lax.ppermute(last, axis, up)
        after = lax.ppermute(leading, axis, down)
        array = jnp.concatenate([before, array, after], axis=dim)
    return array


def shifted(array, axis, by):
    size = lax.axis_size(axis)
    pairs = [(i, i + by) for i in range(size) if 0 <= i + by < size]
    return lax.ppermute(array, axis, pairs)


def product(left, right, pattern):
    return jnp.einsum(pattern, left, right, preferred_element_type=jnp.float32)


def norm_forward(values, gain):
    centred = values - jnp.mean(values, axis=-1, keepdims=True)
    inverse = lax.rsqrt(jnp.mean(centred * centred, axis=-1, keepdims=True) + EPSILON)
    scaled = centred * inverse
    return (scaled * gain, (scaled, inverse))


def norm_backward(grad, kept, gain):
    scaled, inverse = kept
    gain_grad = jnp.sum(grad * scaled, axis=0)
    weighted = grad * gain
    inner = (
        weighted
        - jnp.mean(weighted, axis=-1, keepdims=True)
        - scaled * jnp.mean(weighted * scaled, axis=-1, keepdims=True)
    )
    return (inverse * inner, gain_grad)


def swish_slope(values):
    sigma = jax.nn.sigmoid(values)
    return sigma * (1.0 + values * (1.0 - sigma))


def rotate(values, cosine, sine):
    half_dim = values.shape[-1] // 2
    first, second = (values[..., :half_dim], values[..., half_dim:])
    cos_rows, sin_rows = (cosine[:, None, :], sine[:, None, :])
    return jnp.concatenate(
        [first * cos_rows - second * sin_rows, second * cos_rows + first * sin_rows], axis=-1
    )


def unrotate(values, cosine, sine):
    half_dim = values.shape[-1] // 2
    first, second = (values[..., :half_dim], values[..., half_dim:])
    cos_rows, sin_rows = (cosine[:, None, :], sine[:, None, :])
    return jnp.concatenate(
        [first * cos_rows + second * sin_rows, second * cos_rows - first * sin_rows], axis=-1
    )


def feed_forward(stream, gain, w_in, w_out):
    normed, kept = norm_forward(stream, gain)
    active = normed.astype(jnp.bfloat16)
    hidden = product(active, w_in, "td,df->tf")
    swish = jax.nn.silu(hidden).astype(jnp.bfloat16)
    return (product(swish, w_out, "tf,fd->td"), (kept, active, hidden, swish))


def feed_backward(grad, cache, gain, w_in, w_out):
    kept, active, hidden, swish = cache
    grad_low = grad.astype(jnp.bfloat16)
    out_grad = product(swish, grad_low, "tf,td->fd")
    swish_grad = product(grad_low, w_out, "td,fd->tf")
    hidden_grad = (swish_grad * swish_slope(hidden)).astype(jnp.bfloat16)
    in_grad = product(active, hidden_grad, "td,tf->df")
    active_grad = product(hidden_grad, w_in, "tf,df->td")
    stream_grad, gain_grad = norm_backward(active_grad, kept, gain)
    return (stream_grad, gain_grad, in_grad, out_grad)


def score_parts(queries, near_pairs, own_key, near_ids):
    heads, head_dim = (queries.shape[1], queries.shape[2])
    model_dim = heads * head_dim
    near_keys = near_pairs[:, :model_dim].reshape(near_pairs.shape[0], heads, head_dim)
    raw = product(queries, near_keys, "qhe,khe->hqk") * head_dim ** (-0.5)
    same = (own_key[:, None] == near_ids[None, :])[None]
    return (raw, same, near_keys)


def attend_forward(stream, gain, w_in, w_out, near_ids, own_key, cosine, sine):
    frame_count = stream.shape[0]
    normed, kept = norm_forward(stream, gain)
    active = normed.astype(jnp.bfloat16)
    model_dim = active.shape[1]
    heads = model_dim // HD
    projected = product(active, w_in, "td,df->tf").reshape(frame_count, 3, heads, HD)
    queries = rotate(projected[:, 0], cosine, sine).astype(jnp.bfloat16)
    keyed = rotate(projected[:, 1], cosine, sine).astype(jnp.bfloat16)
    valued = projected[:, 2].astype(jnp.bfloat16)
    paired = jnp.concatenate(
        [keyed.reshape(frame_count, model_dim), valued.reshape(frame_count, model_dim)], axis=1
    )
    near_pairs = extended_2(paired, (("tm", 0),), frame_count)
    raw, same, near_keys = score_parts(queries, near_pairs, own_key, near_ids)
    masked = jnp.where(same, raw, MASKED)
    highest = jnp.max(masked, axis=-1)
    total = jnp.sum(jnp.where(same, jnp.exp(masked - highest[..., None]), 0.0), axis=-1)
    log_total = highest + jnp.log(total)
    weights = jnp.where(same, jnp.exp(raw - log_total[..., None]), 0.0).astype(jnp.bfloat16)
    near_values = near_pairs[:, model_dim:].reshape(near_pairs.shape[0], heads, HD)
    attended = product(weights, near_values, "hqk,khe->qhe")
    rounded = attended.reshape(frame_count, model_dim).astype(jnp.bfloat16)
    result = product(rounded, w_out, "td,de->te")
    return (result, (kept, active, queries, paired, None, log_total, attended, rounded))


def attend_backward(grad, cache, gain, w_in, w_out, near_ids, own_key, cosine, sine):
    kept, active, queries, paired, stored, log_total, attended, rounded = cache
    frame_count, heads, head_dim = queries.shape
    model_dim = heads * head_dim
    scale = head_dim ** (-0.5)
    grad_low = grad.astype(jnp.bfloat16)
    out_grad = product(rounded, grad_low, "td,te->de")
    grad_attended = (
        product(grad_low, w_out, "te,de->td")
        .astype(jnp.bfloat16)
        .reshape(frame_count, heads, head_dim)
    )
    delta = jnp.sum(grad_attended.astype(jnp.float32) * attended, axis=-1).T
    near_pairs = extended_2(paired, (("tm", 0),), frame_count)
    raw, same, near_keys = score_parts(queries, near_pairs, own_key, near_ids)
    weights = jnp.where(same, jnp.exp(raw - log_total[..., None]), 0.0)
    near_values = near_pairs[:, model_dim:].reshape(near_pairs.shape[0], heads, head_dim)
    weight_grad = product(grad_attended, near_values, "qhe,khe->hqk")
    score_grad = (weights * (weight_grad - delta[..., None])).astype(jnp.bfloat16)
    query_grad = product(score_grad, near_keys, "hqk,khe->qhe") * scale
    key_term = (
        product(score_grad, queries, "hqk,qhe->khe").reshape(near_pairs.shape[0], model_dim) * scale
    )
    value_term = product(weights.astype(jnp.bfloat16), grad_attended, "hqk,qhe->khe").reshape(
        near_pairs.shape[0], model_dim
    )
    near_grads = jnp.concatenate([key_term, value_term], axis=1)
    lower_part = near_grads[:frame_count]
    middle_part = near_grads[frame_count : 2 * frame_count]
    upper_part = near_grads[2 * frame_count :]
    from_below = shifted(upper_part.astype(jnp.bfloat16), "tm", 1).astype(upper_part.dtype)
    from_above = shifted(lower_part.astype(jnp.bfloat16), "tm", -1).astype(lower_part.dtype)
    own_grads = middle_part + from_below + from_above
    key_grad = own_grads[:, :model_dim].reshape(frame_count, heads, head_dim)
    value_grad = own_grads[:, model_dim:].reshape(frame_count, heads, head_dim)
    proj_grad = jnp.stack(
        [unrotate(query_grad, cosine, sine), unrotate(key_grad, cosine, sine), value_grad], axis=1
    )
    proj_grad = proj_grad.reshape(frame_count, 3 * model_dim).astype(jnp.bfloat16)
    in_grad = product(active, proj_grad, "td,tf->df")
    active_grad = product(proj_grad, w_in, "tf,df->td")
    stream_grad, gain_grad = norm_backward(active_grad, kept, gain)
    return (stream_grad, gain_grad, in_grad, out_grad)


def conv_forward(
    stream, gain, w_in, w_depth, mean_stat, var_stat, bn_gain, bn_bias, w_out, tap_mask
):
    frame_count, model_dim = stream.shape
    normed, kept = norm_forward(stream, gain)
    active = normed.astype(jnp.bfloat16)
    upper = product(active, w_in, "td,df->tf")
    sigma = jax.nn.sigmoid(upper[:, model_dim:])
    gated = (upper[:, :model_dim] * sigma).astype(jnp.bfloat16)
    extended = extended_2(gated, (("tm", 0),), HALO).astype(jnp.float32)
    depth = jnp.zeros((frame_count, model_dim), jnp.float32)
    for offset in range(KERNEL):
        depth = (
            depth
            + w_depth[offset] * extended[offset : offset + frame_count] * tap_mask[offset][:, None]
        )
    inverse = lax.rsqrt(var_stat + EPSILON)
    centred = (depth - mean_stat) * inverse
    normal_pre = centred * bn_gain + bn_bias
    swish = jax.nn.silu(normal_pre).astype(jnp.bfloat16)
    return (
        product(swish, w_out, "td,de->te"),
        (kept, active, upper, sigma, extended, inverse, centred, normal_pre, swish),
    )


def conv_backward(grad, cache, gain, w_in, w_depth, bn_gain, w_out, tap_mask):
    kept, active, upper, sigma, extended, inverse, centred, normal_pre, swish = cache
    frame_count, model_dim = grad.shape
    grad_low = grad.astype(jnp.bfloat16)
    out_grad = product(swish, grad_low, "td,te->de")
    swish_grad = product(grad_low, w_out, "te,de->td")
    pre_grad = swish_grad * swish_slope(normal_pre)
    scale_grad = jnp.sum(pre_grad * centred, axis=0)
    shift_grad = jnp.sum(pre_grad, axis=0)
    depth_grad = (pre_grad * bn_gain * inverse).astype(jnp.bfloat16)
    grad_ext = extended_2(depth_grad, (("tm", 0),), HALO).astype(jnp.float32)
    depth_wide = depth_grad.astype(jnp.float32)
    tap_grads = []
    gated_grad = jnp.zeros((frame_count, model_dim), jnp.float32)
    for offset in range(KERNEL):
        tap_grads.append(
            jnp.sum(
                depth_wide * extended[offset : offset + frame_count] * tap_mask[offset][:, None],
                axis=0,
            )
        )
        gated_grad = (
            gated_grad
            + w_depth[KERNEL - 1 - offset]
            * grad_ext[offset : offset + frame_count]
            * tap_mask[offset][:, None]
        )
    lower_grad = gated_grad * sigma
    gate_grad = gated_grad * upper[:, :model_dim] * sigma * (1.0 - sigma)
    upper_grad = jnp.concatenate([lower_grad, gate_grad], axis=1).astype(jnp.bfloat16)
    in_grad = product(active, upper_grad, "td,tf->df")
    active_grad = product(upper_grad, w_in, "tf,df->td")
    stream_grad, gain_grad = norm_backward(active_grad, kept, gain)
    return (stream_grad, gain_grad, in_grad, jnp.stack(tap_grads), scale_grad, shift_grad, out_grad)


def layer_forward(stream, weights, near_ids, own_key, tap_mask, cosine, sine):
    (
        gain_rows,
        w_feed_in,
        w_feed_out,
        w_attend_in,
        w_attend_out,
        w_point_in,
        w_depth,
        mean_stat,
        var_stat,
        bn_gain,
        bn_bias,
        w_point_out,
    ) = weights
    first_out, first_cache = feed_forward(stream, gain_rows[0], w_feed_in[0], w_feed_out[0])
    stream = stream + 0.5 * first_out
    attend_res, attend_cache = attend_forward(
        stream, gain_rows[1], w_attend_in, w_attend_out, near_ids, own_key, cosine, sine
    )
    stream = stream + attend_res
    conv_res, conv_cache = conv_forward(
        stream,
        gain_rows[2],
        w_point_in,
        w_depth,
        mean_stat,
        var_stat,
        bn_gain,
        bn_bias,
        w_point_out,
        tap_mask,
    )
    stream = stream + conv_res
    second_out, second_cache = feed_forward(stream, gain_rows[3], w_feed_in[1], w_feed_out[1])
    stream = stream + 0.5 * second_out
    result, final_kept = norm_forward(stream, gain_rows[4])
    return (result, (first_cache, attend_cache, conv_cache, second_cache, final_kept))


def layer_backward(grad, caches, weights, near_ids, own_key, tap_mask, cosine, sine):
    (
        gain_rows,
        w_feed_in,
        w_feed_out,
        w_attend_in,
        w_attend_out,
        w_point_in,
        w_depth,
        mean_stat,
        var_stat,
        bn_gain,
        bn_bias,
        w_point_out,
    ) = weights
    first_cache, attend_cache, conv_cache, second_cache, final_kept = caches
    grad, final_gain = norm_backward(grad, final_kept, gain_rows[4])
    branch, second_gain, second_in, second_out = feed_backward(
        0.5 * grad, second_cache, gain_rows[3], w_feed_in[1], w_feed_out[1]
    )
    grad = grad + branch
    branch, conv_gain, point_in_grad, depth_grad, scale_grad, shift_grad, point_out_grad = (
        conv_backward(
            grad, conv_cache, gain_rows[2], w_point_in, w_depth, bn_gain, w_point_out, tap_mask
        )
    )
    grad = grad + branch
    branch, attend_gain, attend_in_grad, attend_out_grad = attend_backward(
        grad, attend_cache, gain_rows[1], w_attend_in, w_attend_out, near_ids, own_key, cosine, sine
    )
    grad = grad + branch
    branch, first_gain, first_in, first_out = feed_backward(
        0.5 * grad, first_cache, gain_rows[0], w_feed_in[0], w_feed_out[0]
    )
    grad = grad + branch
    gains_grad = jnp.stack([first_gain, attend_gain, conv_gain, second_gain, final_gain])
    grads = (
        gains_grad,
        jnp.stack([first_in, second_in]),
        jnp.stack([first_out, second_out]),
        attend_in_grad,
        attend_out_grad,
        point_in_grad,
        depth_grad,
        scale_grad,
        shift_grad,
        point_out_grad,
    )
    return (grad, grads)


def per_device(
    frames,
    segment_ids,
    norm_gains,
    feed_in,
    feed_out,
    attend_in,
    attend_out,
    point_in,
    depthwise,
    stat_mean,
    stat_var,
    batch_scale,
    batch_shift,
    point_out,
    cotangent,
):
    batches, row_count, frame_count, model_dim = frames.shape
    layer_count = norm_gains.shape[0]
    half_dim = HD // 2
    frequency = 10000.0 ** (-jnp.arange(half_dim).astype(jnp.float32) / half_dim)
    all_near = extended_2(segment_ids + 1, (("tm", 2),), frame_count)
    indices = jnp.arange(3 * frame_count)
    totals = [None] * layer_count
    outputs = []
    input_grads = []
    for batch_index in range(batches):
        near_ids = all_near[batch_index, 0]
        own_key = near_ids[frame_count : 2 * frame_count]
        starts_here = jnp.concatenate([jnp.ones((1,), jnp.bool_), near_ids[1:] != near_ids[:-1]])
        opening = lax.cummax(jnp.where(starts_here, indices, 0), axis=0)
        position = (indices - opening)[frame_count : 2 * frame_count].astype(jnp.float32)
        angle = position[:, None] * frequency[None, :]
        cosine = jnp.cos(angle)
        sine = jnp.sin(angle)
        window = near_ids[frame_count - HALO : 2 * frame_count + HALO]
        tap_mask = jnp.stack(
            [window[offset : offset + frame_count] == own_key for offset in range(KERNEL)]
        ).astype(jnp.float32)
        stream = frames[batch_index, 0].astype(jnp.float32)
        layer_list = []
        caches = []
        for layer_index in range(layer_count):
            weights = (
                norm_gains[layer_index],
                feed_in[layer_index],
                feed_out[layer_index],
                attend_in[layer_index],
                attend_out[layer_index],
                point_in[layer_index],
                depthwise[layer_index],
                stat_mean[layer_index],
                stat_var[layer_index],
                batch_scale[layer_index],
                batch_shift[layer_index],
                point_out[layer_index],
            )
            layer_list.append(weights)
            stream, cache = layer_forward(
                stream, weights, near_ids, own_key, tap_mask, cosine, sine
            )
            caches.append(cache)
        outputs.append(stream.astype(jnp.bfloat16))
        grad = cotangent[batch_index, 0].astype(jnp.float32)
        for layer_index in reversed(range(layer_count)):
            grad, grads = layer_backward(
                grad,
                caches[layer_index],
                layer_list[layer_index],
                near_ids,
                own_key,
                tap_mask,
                cosine,
                sine,
            )
            if totals[layer_index] is None:
                totals[layer_index] = grads
            else:
                totals[layer_index] = tuple(
                    (left + right for left, right in zip(totals[layer_index], grads))
                )
        input_grads.append(grad.astype(jnp.bfloat16))
    stacked = tuple(
        (
            jnp.stack([totals[layer_index][member] for layer_index in range(layer_count)])
            for member in range(10)
        )
    )
    summed = (
        lax.psum_scatter(stacked[0], "tm", scatter_dimension=2, tiled=True),
        lax.psum_scatter(stacked[1], "tm", scatter_dimension=3, tiled=True),
        lax.psum_scatter(stacked[2], "tm", scatter_dimension=3, tiled=True),
        lax.psum_scatter(stacked[3], "tm", scatter_dimension=2, tiled=True),
        lax.psum_scatter(stacked[4], "tm", scatter_dimension=2, tiled=True),
        lax.psum_scatter(stacked[5], "tm", scatter_dimension=2, tiled=True),
        lax.psum_scatter(stacked[6], "tm", scatter_dimension=2, tiled=True),
        lax.psum_scatter(stacked[7], "tm", scatter_dimension=1, tiled=True),
        lax.psum_scatter(stacked[8], "tm", scatter_dimension=1, tiled=True),
        lax.psum_scatter(stacked[9], "tm", scatter_dimension=2, tiled=True),
    )
    small_sums = lax.psum((summed[0], summed[6], summed[7], summed[8]), "rows")
    row_shares = (
        lax.psum_scatter(
            summed[1].astype(jnp.bfloat16), "rows", scatter_dimension=2, tiled=True
        ).astype(jnp.float32),
        lax.psum_scatter(
            summed[2].astype(jnp.bfloat16), "rows", scatter_dimension=2, tiled=True
        ).astype(jnp.float32),
        lax.psum_scatter(
            summed[3].astype(jnp.bfloat16), "rows", scatter_dimension=1, tiled=True
        ).astype(jnp.float32),
        lax.psum_scatter(
            summed[4].astype(jnp.bfloat16), "rows", scatter_dimension=1, tiled=True
        ).astype(jnp.float32),
        lax.psum_scatter(
            summed[5].astype(jnp.bfloat16), "rows", scatter_dimension=1, tiled=True
        ).astype(jnp.float32),
        lax.psum_scatter(
            summed[9].astype(jnp.bfloat16), "rows", scatter_dimension=1, tiled=True
        ).astype(jnp.float32),
    )
    matrix_sums = (
        lax.all_gather(row_shares[0].astype(jnp.bfloat16), "rows", axis=2, tiled=True).astype(
            jnp.float32
        ),
        lax.all_gather(row_shares[1].astype(jnp.bfloat16), "rows", axis=2, tiled=True).astype(
            jnp.float32
        ),
        lax.all_gather(row_shares[2].astype(jnp.bfloat16), "rows", axis=1, tiled=True).astype(
            jnp.float32
        ),
        lax.all_gather(row_shares[3].astype(jnp.bfloat16), "rows", axis=1, tiled=True).astype(
            jnp.float32
        ),
        lax.all_gather(row_shares[4].astype(jnp.bfloat16), "rows", axis=1, tiled=True).astype(
            jnp.float32
        ),
        lax.all_gather(row_shares[5].astype(jnp.bfloat16), "rows", axis=1, tiled=True).astype(
            jnp.float32
        ),
    )
    activations = jnp.stack(outputs).reshape(batches, row_count, frame_count, model_dim)
    frames_grad = jnp.stack(input_grads).reshape(batches, row_count, frame_count, model_dim)
    return (
        activations,
        frames_grad,
        small_sums[0],
        matrix_sums[0],
        matrix_sums[1],
        matrix_sums[2],
        matrix_sums[3],
        matrix_sums[4],
        small_sums[1],
        small_sums[2],
        small_sums[3],
        matrix_sums[5],
    )


def solution(mesh):
    in_specs = (
        P(None, "rows", "tm", None),
        P(None, "rows", "tm"),
        P(),
        P(),
        P(),
        P(),
        P(),
        P(),
        P(),
        P(),
        P(),
        P(),
        P(),
        P(),
        P(None, "rows", "tm", None),
    )
    out_specs = (
        P(None, "rows", "tm", None),
        P(None, "rows", "tm", None),
        P(None, None, "tm"),
        P(None, None, None, "tm"),
        P(None, None, None, "tm"),
        P(None, None, "tm"),
        P(None, None, "tm"),
        P(None, None, "tm"),
        P(None, None, "tm"),
        P(None, "tm"),
        P(None, "tm"),
        P(None, None, "tm"),
    )
    return jax.shard_map(
        per_device, mesh=mesh, in_specs=in_specs, out_specs=out_specs, check_vma=False
    )
```

profile of v0, /device:TPU:10, one launch (start us, length us, event | category | flops | bytes accessed | tf_op | source)
XLA Modules:
  0.0 1952.4 jit_solution(9700073159032175086)
XLA Ops:
  245.5 5.3 collective-permute-done.10
  534.2 13.7 fusion.3
  628.6 15.1 fusion.1
  643.8 9.7 pad_maximum_fusion
  711.3 11.5 fusion.7
  736.0 10.6 copy.90
  755.2 15.5 fusion.5
  770.7 10.0 pad_maximum_fusion.1
  780.7 25.7 %copy.89 = f32[2,2,2048,512]{2,1,0,3:T(2,128)} copy(f32[2,2,2048,512]{3,2,1,0:T(8,128)} %pad_maximum_fusion.1) | data formatting | bytes 33554432 | tf_op jit(solution)/shard_map/stack | solution.py:418
  806.4 530.3 %all-reduce.7 = (bf16[2,2,2048,512]{2,1,0,3:T(2,128)(2,1)}, bf16[2,512,1536]{1,0,2:T(2,128)(2,1)}, bf16[2,512,512]{1,0,2:T(2,128)(2,1)}, bf16[2,512,512]{1,0,2:T(2,128)(2,1)}) all-reduce(f32[2,2,2048,512]{2,1,0,3:T(2,128)} %copy.89, f32[2,512,1536]{1,0,2:T(2,128)} %copy.90, ...), channel_id=5, replica_groups=mesh['rows'=4,'tm'=8] {'tm'}, use_global_device_ids=true, to_apply=%region_236.237.clone | all-reduce | flops 6815744 | bytes 40894464
  1338.9 104.4 %copy.109 = bf16[2,2,2048,64]{1,0,3,2:T(2,128)(2,1)} copy(bf16[2,2,2048,64]{2,1,0,3:T(2,128)(2,1)S(1)} %dynamic-slice_convert_fusion) | data formatting | bytes 2097152
  1443.3 97.2 %reshape.4701 = bf16[2048,256]{1,0:T(8,128)(2,1)} reshape(bf16[2048,64,2,2]{3,2,1,0:T(2,128)(2,1)} %bitcast.500) | data formatting | bytes 2097152
  1585.9 13.7 copy.121
  1599.6 13.7 reshape.4713
  1614.4 13.7 copy.113
  1628.2 13.7 reshape.4705
  1643.8 18.7 copy.111
  1662.5 35.1 %reshape.4703 = bf16[512,384]{1,0:T(8,128)(2,1)} reshape(bf16[512,192,2]{2,1,0:T(8,128)(2,1)} %bitcast.1531) | data formatting | bytes 786432
  1697.9 37.9 %reshape.4702 = bf16[512,64,2,2]{3,2,1,0:T(2,128)(2,1)} reshape(bf16[512,256]{1,0:T(8,128)(2,1)} %reduce-scatter.39.cloned.1.call-done) | data formatting | bytes 524288
  1735.8 34.4 %copy.110 = bf16[2,2,512,64]{2,1,0,3:T(2,128)(2,1)} copy(bf16[2,2,512,64]{1,0,3,2:T(2,128)(2,1)} %bitcast.1532) | data formatting | bytes 524288
  1778.6 14.7 all-reduce.5
  1793.3 8.7 reduce-scatter.51.cloned.1.call-done
  1809.5 8.2 all_gather.23
  1818.4 10.3 reduce-scatter.43.cloned.1.call-done
  1836.1 9.0 all_gather.21
  1845.9 10.8 reduce-scatter.41.cloned.1.call-done
  1856.7 14.8 reshape.4704
  1871.5 6.4 copy.112
  1877.9 12.9 all_gather.20
  1895.0 19.3 reduce-scatter.35.cloned.1.call-done
  1914.4 8.3 all_gather.22
  1923.5 19.4 all-gather.3.cloned.1.call-done
  (3179 shorter events, 746.8 us)
Async XLA Ops:
  7.2 1568.7 %reduce-scatter.29.cloned.1.call-start = ((), (), s32[]{:S(2)}) async-start(), calls=%async_computation.12 | async-start | bytes 18874368 | tf_op jit(solution)/shard_map/reduce_scatter | solution.py:424
  7.9 30.3 %collective-permute-start.1 = (s32[4,1,128]{2,1,0:T(1,128)S(1)}, s32[4,1,128]{2,1,0:T(1,128)S(1)}, u32[]{:S(2)}, u32[]{:S(2)}) collective-permute-start(s32[4,1,128]{2,1,0:T(1,128)S(1)} %broadcast_add_fusion), channel_id=1, source_target_pairs={{1,0},{2,1},{3,2},{4,3},{5,4},{6,5},{7,6},{9,8},{10,9},{11,10},{12... | collective-permute-start | bytes 6152 | tf_op jit(solution)/shard_map/ppermute | solution.py:23
  9.8 28.4 %collective-permute-start = (s32[4,1,128]{2,1,0:T(1,128)S(1)}, s32[4,1,128]{2,1,0:T(1,128)S(1)}, u32[]{:S(2)}, u32[]{:S(2)}) collective-permute-start(s32[4,1,128]{2,1,0:T(1,128)S(1)} %broadcast_add_fusion), channel_id=1, source_target_pairs={{0,1},{1,2},{2,3},{3,4},{4,5},{5,6},{6,7},{8,9},{9,10},{10,11},{11... | collective-permute-start | bytes 6152 | tf_op jit(solution)/shard_map/ppermute | solution.py:22
  218.6 24.4 %collective-permute-start.27 = (bf16[128,1024]{0,1:T(8,128)(2,1)S(1)}, bf16[128,1024]{0,1:T(8,128)(2,1)S(1)}, u32[]{:S(2)}, u32[]{:S(2)}) collective-permute-start(bf16[128,1024]{0,1:T(8,128)(2,1)S(1)} %pad_maximum_fusion.28), channel_id=1, source_target_pairs={{1,0},{2,1},{3,2},{4,3},{5,4},{6,5},{7,6},{9,8},{10,9},{11,10},{12... | collective-permute-start | bytes 786440 | tf_op jit(solution)/shard_map/ppermute | solution.py:23
  222.4 22.5 %collective-permute-start.26 = (bf16[128,1024]{0,1:T(8,128)(2,1)S(1)}, bf16[128,1024]{0,1:T(8,128)(2,1)S(1)}, u32[]{:S(2)}, u32[]{:S(2)}) collective-permute-start(bf16[128,1024]{0,1:T(8,128)(2,1)S(1)} %pad_maximum_fusion.28), channel_id=1, source_target_pairs={{0,1},{1,2},{2,3},{3,4},{4,5},{5,6},{6,7},{8,9},{9,10},{10,11},{11... | collective-permute-start | bytes 786440 | tf_op jit(solution)/shard_map/ppermute | solution.py:22
  227.7 17.5 collective-permute-start.3
  254.4 20.4 %collective-permute-start.12 = (bf16[4,512]{1,0:T(4,128)(2,1)S(1)}, bf16[4,512]{1,0:T(4,128)(2,1)S(1)}, u32[]{:S(2)}, u32[]{:S(2)}) collective-permute-start(bf16[4,512]{1,0:T(4,128)(2,1)S(1)} %get-tuple-element.484), channel_id=1, source_target_pairs={{0,1},{1,2},{2,3},{3,4},{4,5},{5,6},{6,7},{8,9},{9,10},{10,11},{11... | collective-permute-start | bytes 12296 | tf_op jit(solution)/shard_map/ppermute | solution.py:22
  256.3 22.3 %collective-permute-start.13 = (bf16[4,512]{1,0:T(4,128)(2,1)S(1)}, bf16[4,512]{1,0:T(4,128)(2,1)S(1)}, u32[]{:S(2)}, u32[]{:S(2)}) collective-permute-start(bf16[4,512]{1,0:T(4,128)(2,1)S(1)} %get-tuple-element.485), channel_id=1, source_target_pairs={{1,0},{2,1},{3,2},{4,3},{5,4},{6,5},{7,6},{9,8},{10,9},{11,10},{12... | collective-permute-start | bytes 12296 | tf_op jit(solution)/shard_map/ppermute | solution.py:23
  263.4 18.2 collective-permute-start.4
  294.9 21.9 %collective-permute-start.31 = (bf16[128,1024]{0,1:T(8,128)(2,1)S(1)}, bf16[128,1024]{0,1:T(8,128)(2,1)S(1)}, u32[]{:S(2)}, u32[]{:S(2)}) collective-permute-start(bf16[128,1024]{0,1:T(8,128)(2,1)S(1)} %pad_maximum_fusion.29), channel_id=1, source_target_pairs={{1,0},{2,1},{3,2},{4,3},{5,4},{6,5},{7,6},{9,8},{10,9},{11,10},{12... | collective-permute-start | bytes 786440 | tf_op jit(solution)/shard_map/ppermute | solution.py:23
  296.8 22.3 %collective-permute-start.30 = (bf16[128,1024]{0,1:T(8,128)(2,1)S(1)}, bf16[128,1024]{0,1:T(8,128)(2,1)S(1)}, u32[]{:S(2)}, u32[]{:S(2)}) collective-permute-start(bf16[128,1024]{0,1:T(8,128)(2,1)S(1)} %pad_maximum_fusion.29), channel_id=1, source_target_pairs={{0,1},{1,2},{2,3},{3,4},{4,5},{5,6},{6,7},{8,9},{9,10},{10,11},{11... | collective-permute-start | bytes 786440 | tf_op jit(solution)/shard_map/ppermute | solution.py:22
  330.5 22.6 %collective-permute-start.8 = (bf16[4,512]{1,0:T(4,128)(2,1)S(1)}, bf16[4,512]{1,0:T(4,128)(2,1)S(1)}, u32[]{:S(2)}, u32[]{:S(2)}) collective-permute-start(bf16[4,512]{1,0:T(4,128)(2,1)S(1)} %get-tuple-element.476), channel_id=1, source_target_pairs={{0,1},{1,2},{2,3},{3,4},{4,5},{5,6},{6,7},{8,9},{9,10},{10,11},{11... | collective-permute-start | bytes 12296 | tf_op jit(solution)/shard_map/ppermute | solution.py:22
  332.4 24.5 %collective-permute-start.9 = (bf16[4,512]{1,0:T(4,128)(2,1)S(1)}, bf16[4,512]{1,0:T(4,128)(2,1)S(1)}, u32[]{:S(2)}, u32[]{:S(2)}) collective-permute-start(bf16[4,512]{1,0:T(4,128)(2,1)S(1)} %get-tuple-element.477), channel_id=1, source_target_pairs={{1,0},{2,1},{3,2},{4,3},{5,4},{6,5},{7,6},{9,8},{10,9},{11,10},{12... | collective-permute-start | bytes 12296 | tf_op jit(solution)/shard_map/ppermute | solution.py:23
  384.9 17.8 collective-permute-start.58
  386.9 19.6 %collective-permute-start.59 = (bf16[4,512]{1,0:T(4,128)(2,1)S(1)}, bf16[4,512]{1,0:T(4,128)(2,1)S(1)}, u32[]{:S(2)}, u32[]{:S(2)}) collective-permute-start(bf16[4,512]{1,0:T(4,128)(2,1)S(1)} %get-tuple-element.473), channel_id=1, source_target_pairs={{1,0},{2,1},{3,2},{4,3},{5,4},{6,5},{7,6},{9,8},{10,9},{11,10},{12... | collective-permute-start | bytes 12296 | tf_op jit(solution)/shard_map/ppermute | solution.py:23
  517.2 32.6 %collective-permute-start.62 = (bf16[4,512]{1,0:T(4,128)(2,1)S(1)}, bf16[4,512]{1,0:T(4,128)(2,1)S(1)}, u32[]{:S(2)}, u32[]{:S(2)}) collective-permute-start(bf16[4,512]{1,0:T(4,128)(2,1)S(1)} %get-tuple-element.468), channel_id=1, source_target_pairs={{0,1},{1,2},{2,3},{3,4},{4,5},{5,6},{6,7},{8,9},{9,10},{10,11},{11... | collective-permute-start | bytes 12296 | tf_op jit(solution)/shard_map/ppermute | solution.py:22
  521.0 32.9 %collective-permute-start.63 = (bf16[4,512]{1,0:T(4,128)(2,1)S(1)}, bf16[4,512]{1,0:T(4,128)(2,1)S(1)}, u32[]{:S(2)}, u32[]{:S(2)}) collective-permute-start(bf16[4,512]{1,0:T(4,128)(2,1)S(1)} %get-tuple-element.469), channel_id=1, source_target_pairs={{1,0},{2,1},{3,2},{4,3},{5,4},{6,5},{7,6},{9,8},{10,9},{11,10},{12... | collective-permute-start | bytes 12296 | tf_op jit(solution)/shard_map/ppermute | solution.py:23
  525.1 29.5 %collective-permute-start.38 = (bf16[4,512]{1,0:T(4,128)(2,1)S(1)}, bf16[4,512]{1,0:T(4,128)(2,1)S(1)}, u32[]{:S(2)}, u32[]{:S(2)}) collective-permute-start(bf16[4,512]{1,0:T(4,128)(2,1)S(1)} %get-tuple-element.464), channel_id=1, source_target_pairs={{0,1},{1,2},{2,3},{3,4},{4,5},{5,6},{6,7},{8,9},{9,10},{10,11},{11... | collective-permute-start | bytes 12296 | tf_op jit(solution)/shard_map/ppermute | solution.py:22
  527.5 27.2 %collective-permute-start.39 = (bf16[4,512]{1,0:T(4,128)(2,1)S(1)}, bf16[4,512]{1,0:T(4,128)(2,1)S(1)}, u32[]{:S(2)}, u32[]{:S(2)}) collective-permute-start(bf16[4,512]{1,0:T(4,128)(2,1)S(1)} %get-tuple-element.465), channel_id=1, source_target_pairs={{1,0},{2,1},{3,2},{4,3},{5,4},{6,5},{7,6},{9,8},{10,9},{11,10},{12... | collective-permute-start | bytes 12296 | tf_op jit(solution)/shard_map/ppermute | solution.py:23
  653.6 1044.3 %reduce-scatter.39.cloned.1.call-start = ((), (), s32[]{:S(2)}) async-start(), calls=%async_computation.19 | async-start | bytes 1310720
  1540.5 229.9 %reduce-scatter.33.cloned.1.call-start = ((), (), s32[]{:S(2)}) async-start(), calls=%async_computation.16 | async-start | bytes 4718592 | tf_op jit(solution)/shard_map/reduce_scatter | solution.py:428
  1549.7 223.6 %reduce-scatter.47.cloned.1.call-start = ((), (), s32[]{:S(2)}) async-start(), calls=%async_computation.23 | async-start | bytes 294912
  1562.2 211.9 %reduce-scatter.49.cloned.1.call-start = ((), (), s32[]{:S(2)}) async-start(), calls=%async_computation.24 | async-start | bytes 294912
  1563.2 211.8 %reduce-scatter.45.cloned.1.call-start = ((), (), s32[]{:S(2)}) async-start(), calls=%async_computation.22 | async-start | bytes 294912
  1570.6 205.5 %reduce-scatter.31.cloned.1.call-start = ((), (), s32[]{:S(2)}) async-start(), calls=%async_computation.13 | async-start | bytes 1310720 | tf_op jit(solution)/shard_map/reduce_scatter | solution.py:436
  1578.8 198.8 %reduce-scatter.37.cloned.1.call-start = ((), (), s32[]{:S(2)}) async-start(), calls=%async_computation.18 | async-start | bytes 294912
  1584.8 217.2 %reduce-scatter.51.cloned.1.call-start = ((), (), s32[]{:S(2)}) async-start(), calls=%async_computation.25 | async-start | bytes 163840
  1613.4 215.4 %reduce-scatter.43.cloned.1.call-start = ((), (), s32[]{:S(2)}) async-start(), calls=%async_computation.21 | async-start | bytes 163840
  1641.8 214.8 %reduce-scatter.41.cloned.1.call-start = ((), (), s32[]{:S(2)}) async-start(), calls=%async_computation.20 | async-start | bytes 491520
  1697.7 194.2 %all-gather.5.cloned.1.call-start = ((), (), s32[]{:S(2)}) async-start(), calls=%async_computation.15 | async-start | bytes 1310720 | tf_op jit(solution)/shard_map/all_gather | solution.py:459
  1770.3 144.1 %reduce-scatter.35.cloned.1.call-start = ((), (), s32[]{:S(2)}) async-start(), calls=%async_computation.17 | async-start | bytes 327680 | tf_op jit(solution)/shard_map/reduce_scatter | solution.py:448
  1772.3 170.6 %all-gather.3.cloned.1.call-start = ((), (), s32[]{:S(2)}) async-start(), calls=%async_computation.14 | async-start | bytes 1310720 | tf_op jit(solution)/shard_map/all_gather | solution.py:456
  (1094 other events, 8436.9 us)
Sparse Core Ops, SparseCore 0:
  653.7 168.6 reduce-scatter.28
  1540.7 29.8 reduce-scatter.38
  1573.0 46.6 reduce-scatter.32
  1621.9 28.3 reduce-scatter.46
  1652.4 28.4 reduce-scatter.48
  1683.1 28.5 reduce-scatter.44
  1715.2 29.3 reduce-scatter.30
  1746.9 26.8 reduce-scatter.36
  1776.5 25.5 reduce-scatter.50
  1804.9 23.8 reduce-scatter.42
  1832.1 24.5 reduce-scatter.40
  1859.0 28.5 all-gather.4
  1890.3 23.9 reduce-scatter.34
  1916.2 26.6 all-gather.2
where the time goes:
time: 1970 us; the launch traced here: 1950 us
  blocking collectives  583 us (30%)
  local copies, waits for them, and re-layouts  565 us (29%)
  matrix products  307 us (16%)
  starting transfers between devices  185 us (9%)
  other arithmetic  182 us (9%)
  waiting for transfers between devices  97.5 us (5%)
  between operations  32.5 us (2%)
    unnamed x1, blocking collectives  530 us
    unnamed x2215, local copies, waits for them, and re-layouts  484 us
    dot_general x240, matrix products, product(): return jnp.einsum(pattern, left, right, preferred_element_type=jnp.float32)  307 us
    ppermute x25, starting transfers between devices, extended_2(): after = lax.ppermute(leading, axis, down)  81.1 us
    ppermute x25, starting transfers between devices, extended_2(): before = lax.ppermute(last, axis, up)  56.5 us
    add x12, other arithmetic, per_device(): left + right  56 us
    ppermute x16, starting transfers between devices, shifted(): return lax.ppermute(array, axis, pairs)  46.1 us
    another operation x4, local copies, waits for them, and re-layouts, per_device(): jnp.stack([totals[layer_index][member] for layer_index in range(layer_cou...  43.3 us
  transfers between devices with their start and end apart: 80, of which 20 were waited for; matrix products, arithmetic and copies ran while one was open for 37% of the time, Pallas kernels for 0%

commit v1 on v0

v1 whole, which is shorter than its diff:
```python
import functools

import jax
import jax.numpy as jnp
import numpy as np
from jax import lax
from jax.experimental import pallas as pl
from jax.experimental.pallas import tpu as pltpu
from jax.sharding import PartitionSpec as P

HD = 64
KERNEL = 9
HALO = 4
EPSILON = 1e-05
MASKED = -1e30
BF = jnp.bfloat16
F32 = jnp.float32
D = 512
FF = 2048
BLK = 128
ROW_CHOICES = (640, 1024)
CAP = ROW_CHOICES[-1]
LANES = 256
PAIRS = D // 128
VMEM_LIMIT = 60 * 2**20
ANY = pl.BlockSpec(memory_space=pl.ANY)
VMEM = pl.BlockSpec(memory_space=pltpu.VMEM)
SMEM = pl.BlockSpec(memory_space=pltpu.SMEM)


def shifted(array, axis, by):
    size = lax.axis_size(axis)
    pairs = [(i, i + by) for i in range(size) if 0 <= i + by < size]
    return lax.ppermute(array, axis, pairs)


def struct(shape, dtype):
    return jax.ShapeDtypeStruct(shape, dtype)


def call(body, ins, outs, scratch, args, flops=0, moved=0, name="kernel"):
    return pl.pallas_call(
        body,
        out_shape=[s for s, _ in outs],
        in_specs=ins,
        out_specs=[b for _, b in outs],
        scratch_shapes=scratch,
        compiler_params=pltpu.CompilerParams(vmem_limit_bytes=VMEM_LIMIT),
        cost_estimate=pl.CostEstimate(flops=int(flops), bytes_accessed=int(moved), transcendentals=0),
        name=name,
    )(*args)


def dot_nn(a, b):
    return jnp.dot(a, b, preferred_element_type=F32)


def dot_nt(a, b):
    return lax.dot_general(a, b, (((1,), (1,)), ((), ())), preferred_element_type=F32)


def dot_tn(a, b):
    return lax.dot_general(a, b, (((0,), (0,)), ((), ())), preferred_element_type=F32)


def sigmoid(v):
    return 0.5 + 0.5 * jnp.tanh(0.5 * v)


def normalise(x):
    c = x - jnp.mean(x, axis=-1, keepdims=True)
    inv = lax.rsqrt(jnp.mean(c * c, axis=-1, keepdims=True) + EPSILON)
    return c * inv, inv


def norm_back(grad, xhat, inv, gain):
    w = grad * gain
    return inv * (
        w - jnp.mean(w, axis=-1, keepdims=True) - xhat * jnp.mean(w * xhat, axis=-1, keepdims=True)
    )


def fold(v):
    return jnp.sum(v.reshape(v.shape[0] // 8, 8, v.shape[1]), axis=0)


def total(v):
    return jnp.sum(v, axis=0, keepdims=True)


def by_rows(n_ref, body):
    low = 0
    for rows in ROW_CHOICES:
        n = n_ref[0]
        cond = n > low
        if rows != CAP:
            cond = cond & (n <= rows)

        @pl.when(cond)
        def _(rows=rows):
            body(rows)

        low = rows


def blocks(rows, step, init=None, size=128):
    def wrapped(i, carry):
        at = pl.ds(pl.multiple_of(i * size, size), size)
        return step(i, at, carry)

    return lax.fori_loop(0, rows // size, wrapped, init if init is not None else jnp.int32(0))


def rope_tables():
    half = HD // 2
    freq = np.power(np.float32(10000.0), -(np.arange(half).astype(np.float32) / np.float32(half)))
    angle = np.arange(BLK).astype(np.float32)[:, None] * freq.astype(np.float32)[None, :]
    cos = np.cos(angle.astype(np.float64))
    sin = np.sin(angle.astype(np.float64))
    full = (np.concatenate([cos] * 4, axis=1), np.concatenate([-sin, sin] * 2, axis=1))
    parts = []
    for table in full:
        rest = table
        for _ in range(3):
            piece = rest.astype(jnp.bfloat16)
            parts.append(piece)
            rest = rest - piece.astype(np.float64)
    return np.stack(parts)


def pack_body(keep_ref, key_ref, keyc_ref, win_ref, tab_ref, x_ref, p_ref, cos_ref, sin_ref, kb_ref, kr_ref, dest_s, pos_s):
    count = keep_ref.shape[1]
    win = count // 4
    keep = keep_ref[...]
    before = (
        lax.broadcasted_iota(jnp.int32, (count, count), 0) < lax.broadcasted_iota(jnp.int32, (count, count), 1)
    ).astype(F32).astype(BF)
    dest = dot_nn(jnp.broadcast_to(keep, (8, count)).astype(BF), before)
    dest_s[...] = jnp.where(jnp.broadcast_to(keep, (8, count)) > 0.5, dest, -1.0)
    earlier = lax.broadcasted_iota(jnp.int32, (win, win), 0) < lax.broadcasted_iota(jnp.int32, (win, win), 1)
    for m in range(4):
        at = pl.ds(m * win, win)
        same = (keyc_ref[at, :] == key_ref[:, at]) & earlier
        pos_s[:, at] = jnp.broadcast_to(jnp.sum(jnp.where(same, 1.0, 0.0), axis=0, keepdims=True), (8, win))
    kr_ref[...] = jnp.full(kr_ref.shape, -1.0, F32)

    def step(i, at, carry):
        row = (lax.broadcasted_iota(jnp.int32, (BLK, count), 0) + i * BLK).astype(F32)
        pick = jnp.where(dest_s[0:1, :] == row, 1.0, 0.0)
        p = pick.astype(BF)
        p_ref[at, :] = p
        x_ref[at, :] = dot_nn(p, win_ref[...])
        key = jnp.broadcast_to(jnp.sum(pick * key_ref[...], axis=1, keepdims=True), (BLK, BLK))
        kb_ref[at, :] = key
        kr_ref[:, pl.ds(pl.multiple_of(i * BLK + BLK, BLK), BLK)] = key.T[0:8]
        pos = jnp.sum(pick * pos_s[0:1, :], axis=1, keepdims=True)
        hot = (lax.broadcasted_iota(jnp.int32, (BLK, BLK), 1).astype(F32) == pos).astype(F32).astype(BF)
        cos_ref[at, :] = dot_nn(hot, tab_ref[0]) + dot_nn(hot, tab_ref[1]) + dot_nn(hot, tab_ref[2])
        sin_ref[at, :] = dot_nn(hot, tab_ref[3]) + dot_nn(hot, tab_ref[4]) + dot_nn(hot, tab_ref[5])
        return carry

    blocks(count, step)


def pack(keep, key, window):
    count = keep.shape[0]
    return call(
        pack_body,
        [VMEM] * 5,
        [
            (struct((CAP, D), F32), VMEM),
            (struct((CAP, count), BF), VMEM),
            (struct((CAP, 128), F32), VMEM),
            (struct((CAP, 128), F32), VMEM),
            (struct((CAP, 128), F32), VMEM),
            (struct((8, CAP + 2 * BLK), F32), VMEM),
        ],
        [pltpu.VMEM((8, count), F32), pltpu.VMEM((8, count), F32)],
        (keep[None, :], key[None, :], key[:, None], window, jnp.asarray(rope_tables(), dtype=BF)),
        flops=2 * count * count * D,
        moved=8 * 2**20,
        name="pack",
    )


def lane_low(shape):
    return lax.broadcasted_iota(jnp.int32, shape, 1) % HD < HD // 2


def swap_halves(v):
    return jnp.where(lane_low(v.shape), pltpu.roll(v, 128 - HD // 2, 1), pltpu.roll(v, HD // 2, 1))


def stacked(v):
    first = lax.broadcasted_iota(jnp.int32, v.shape, 1) < HD
    zero = jnp.zeros_like(v)
    return jnp.concatenate([jnp.where(first, v, zero), jnp.where(first, zero, v)], axis=0)


def unstacked(v):
    half = v.shape[0] // 2
    first = lax.broadcasted_iota(jnp.int32, (half, 128), 1) < HD
    return jnp.where(first, v[:half], v[half:])


def norm_into(x_ref, gain, a_ref, rows):
    def step(i, at, carry):
        xhat, _ = normalise(x_ref[at, :])
        a_ref[at, :] = (xhat * gain).astype(BF)
        return carry

    blocks(rows, step)


def forward_body(
    n_ref, x0_ref, cos_ref, sin_ref, kb_ref, kr_ref, gains_ref, taps_ref, mean_ref, var_ref, scale_ref, shift_ref,
    fin_h, fout_h, ain_h, aout_h, pin_h, pout_h,
    act_ref, xs_h, hs_h, q_h, kv_h, at_h, o_h, u_h, z_h,
    fin, fout, ain, aout, pin, pout, xb, hb, qb, kvb, ab, ob, ub, zb, a_s, gp, kp, w_sem, s_sem,
):
    layers = gains_ref.shape[0]
    weights = [
        (fin_h, (0,), fin.at[0]), (fout_h, (0,), fout.at[0]), (ain_h, (), ain), (aout_h, (), aout),
        (pin_h, (), pin), (pout_h, (), pout), (fin_h, (1,), fin.at[1]), (fout_h, (1,), fout.at[1]),
    ]

    def weight_copy(i, l):
        src, sub, dst = weights[i]
        return pltpu.make_async_copy(src.at[(l,) + sub], dst, w_sem.at[i])

    for i in range(len(weights)):
        weight_copy(i, 0).start()

    def run(rows):
        tiles = rows // BLK
        top = pl.ds(0, rows)
        saves = [(xb.at[i, top], lambda l, i=i: xs_h.at[l, i, top]) for i in range(5)]
        saves += [(hb.at[k, top], lambda l, k=k: hs_h.at[l, k, top]) for k in range(2)]
        saves += [
            (qb.at[top], lambda l: q_h.at[l, top]),
            (kvb.at[pl.ds(0, rows + 2 * BLK)], lambda l: kv_h.at[l, pl.ds(0, rows + 2 * BLK)]),
            (ab.at[pl.ds(0, tiles)], lambda l: at_h.at[l, pl.ds(0, tiles)]),
            (ob.at[top], lambda l: o_h.at[l, top]),
            (ub.at[top], lambda l: u_h.at[l, top]),
            (zb.at[top], lambda l: z_h.at[l, top]),
        ]

        def save(i, l):
            src, dst = saves[i]
            return pltpu.make_async_copy(src, dst(l), s_sem.at[i])

        def settle(i, l):
            @pl.when(l > 0)
            def _():
                save(i, l - 1).wait()

        def use(i, l):
            weight_copy(i, l).wait()

        def next_weight(i, l):
            @pl.when(l + 1 < layers)
            def _():
                weight_copy(i, l + 1).start()

        kvb[pl.ds(0, BLK), :] = jnp.zeros((BLK, 2 * D), BF)
        kvb[pl.ds(rows + BLK, BLK), :] = jnp.zeros((BLK, 2 * D), BF)
        gp[pl.ds(0, 8), :] = jnp.zeros((8, D), F32)
        gp[pl.ds(rows + 8, 8), :] = jnp.zeros((8, D), F32)
        kp[pl.ds(0, 8), :] = jnp.full((8, 128), -1.0, F32)
        kp[pl.ds(rows + 8, 8), :] = jnp.full((8, 128), -1.0, F32)

        def fill(i, at, carry):
            kp[pl.ds(pl.multiple_of(i * BLK + 8, 8), BLK), :] = kb_ref[at, :]
            xb[0, at, :] = x0_ref[at, :]
            return carry

        blocks(rows, fill)

        def feed(l, k, src, dst, gain, wi):
            settle(5 + k, l)
            settle(dst, l)

            def first(i, at, carry):
                x = xb[src, at, :]
                xhat, _ = normalise(x)
                a_s[at, :] = (xhat * gain).astype(BF)
                xb[dst, at, :] = x
                return carry

            blocks(rows, first)
            use(wi, l)
            use(wi + 1, l)

            def chunk(c, carry):
                cols = pl.ds(pl.multiple_of(c * 512, 512), 512)
                h = dot_nn(a_s[top, :], fin[k, :, cols])
                hb[k, top, cols] = h.astype(BF)
                s = (h * sigmoid(h)).astype(BF)
                xb[dst, top, :] = xb[dst, top, :] + 0.5 * dot_nn(s, fout[k, cols, :])
                return carry

            lax.fori_loop(0, FF // 512, chunk, jnp.int32(0))
            next_weight(wi, l)
            next_weight(wi + 1, l)
            save(5 + k, l).start()
            save(dst, l).start()

        def layer(l, carry):
            gains = [gains_ref[l, pl.ds(i, 1), :] for i in range(5)]
            save(0, l).start()
            feed(l, 0, 0, 1, gains[0], 0)

            norm_into(xb.at[1], gains[1], a_s, rows)
            settle(7, l)
            settle(8, l)
            settle(9, l)
            settle(10, l)
            use(2, l)
            for part in range(3):
                proj = dot_nn(a_s[top, :], ain[:, part * D : (part + 1) * D])
                for p in range(PAIRS):
                    lanes = slice(p * 128, (p + 1) * 128)
                    v = proj[:, lanes]
                    if part < 2:
                        v = v * cos_ref[top, :] + swap_halves(v) * sin_ref[top, :]
                    if part == 0:
                        qb[top, lanes] = (v * HD**-0.5).astype(BF)
                    elif part == 1:
                        kvb[pl.ds(BLK, rows), lanes] = v.astype(BF)
                    else:
                        kvb[pl.ds(BLK, rows), D + p * 128 : D + (p + 1) * 128] = v.astype(BF)
            next_weight(2, l)

            def tile(t, at, c):
                near = pl.ds(pl.multiple_of(t * BLK, BLK), 3 * BLK)
                same = kb_ref[at, 0:1] == kr_ref[0:1, near]
                same = jnp.concatenate([same, same], axis=0)
                for p in range(PAIRS):
                    lanes = slice(p * 128, (p + 1) * 128)
                    s = dot_nt(stacked(qb[at, lanes]), kvb[near, lanes])
                    s = jnp.where(same, s, MASKED)
                    e = jnp.exp(s - jnp.max(s, axis=-1, keepdims=True))
                    e = e / jnp.sum(e, axis=-1, keepdims=True)
                    low = e.astype(BF)
                    ab[t, p] = low
                    o = dot_nn(low, kvb[near, D + p * 128 : D + (p + 1) * 128])
                    ob[at, lanes] = unstacked(o).astype(BF)
                return c

            blocks(rows, tile)
            settle(2, l)
            use(3, l)
            xb[2, top, :] = xb[1, top, :] + dot_nn(ob[top, :], aout[...])
            next_weight(3, l)
            for i in (7, 8, 9, 10, 2):
                save(i, l).start()

            norm_into(xb.at[2], gains[2], a_s, rows)
            settle(11, l)
            settle(12, l)
            use(4, l)
            for half in range(2):
                lanes = slice(half * 256, (half + 1) * 256)
                up1 = dot_nn(a_s[top, :], pin[:, half * 256 : (half + 1) * 256])
                up2 = dot_nn(a_s[top, :], pin[:, D + half * 256 : D + (half + 1) * 256])
                ub[top, lanes] = up1.astype(BF)
                ub[top, D + half * 256 : D + (half + 1) * 256] = up2.astype(BF)
                gp[pl.ds(8, rows), lanes] = (up1 * sigmoid(up2)).astype(BF).astype(F32)
            next_weight(4, l)
            rs = lax.rsqrt(var_ref[pl.ds(l, 1), :] + EPSILON)
            mean = mean_ref[pl.ds(l, 1), :]
            scale = scale_ref[pl.ds(l, 1), :]
            shift = shift_ref[pl.ds(l, 1), :]

            def conv(t, at, c):
                wide = pl.ds(pl.multiple_of(t * BLK, BLK), BLK + 16)
                keys = kp[wide, :]
                own = keys[8 : 8 + BLK]
                masks = [keys[4 + o : 4 + o + BLK] == own for o in range(KERNEL)]
                for p in range(PAIRS):
                    lanes = slice(p * 128, (p + 1) * 128)
                    g = gp[wide, lanes]
                    z = jnp.zeros((BLK, 128), F32)
                    for o in range(KERNEL):
                        w = taps_ref[l, o : o + 1, lanes]
                        z = z + jnp.where(masks[o], w * g[4 + o : 4 + o + BLK], 0.0)
                    zb[at, lanes] = z
                    b = (z - mean[:, lanes]) * rs[:, lanes] * scale[:, lanes] + shift[:, lanes]
                    a_s[at, lanes] = (b * sigmoid(b)).astype(BF)
                return c

            blocks(rows, conv)
            settle(3, l)
            use(5, l)
            xb[3, top, :] = xb[2, top, :] + dot_nn(a_s[top, :], pout[...])
            next_weight(5, l)
            for i in (11, 12, 3):
                save(i, l).start()

            feed(l, 1, 3, 4, gains[3], 6)
            save(0, l).wait()

            def last(i, at, c):
                xhat, _ = normalise(xb[4, at, :])
                y = xhat * gains[4]
                xb[0, at, :] = y
                act_ref[at, :] = y.astype(BF)
                return c

            blocks(rows, last)
            return carry

        lax.fori_loop(0, layers, layer, jnp.int32(0))
        for i in range(1, len(saves)):
            save(i, layers - 1).wait()
        if rows < CAP:
            act_ref[pl.ds(rows, CAP - rows), :] = jnp.zeros((CAP - rows, D), BF)

    by_rows(n_ref, run)


def forward(n, x0, cos, sin, kb, kr, small, mats):
    layers = small[0].shape[0]
    outs = [
        (struct((CAP, D), BF), VMEM),
        (struct((layers, 5, CAP, D), F32), ANY),
        (struct((layers, 2, CAP, FF), BF), ANY),
        (struct((layers, CAP, D), BF), ANY),
        (struct((layers, CAP + 2 * BLK, 2 * D), BF), ANY),
        (struct((layers, CAP // BLK, PAIRS, 2 * BLK, 3 * BLK), BF), ANY),
        (struct((layers, CAP, D), BF), ANY),
        (struct((layers, CAP, 2 * D), BF), ANY),
        (struct((layers, CAP, D), F32), ANY),
    ]
    vm = pltpu.VMEM
    scratch = [
        vm((2, D, FF), BF), vm((2, FF, D), BF), vm((D, 3 * D), BF), vm((D, D), BF), vm((D, 2 * D), BF), vm((D, D), BF),
        vm((5, CAP, D), F32), vm((2, CAP, FF), BF), vm((CAP, D), BF), vm((CAP + 2 * BLK, 2 * D), BF),
        vm((CAP // BLK, PAIRS, 2 * BLK, 3 * BLK), BF), vm((CAP, D), BF), vm((CAP, 2 * D), BF), vm((CAP, D), F32),
        vm((CAP, D), BF), vm((CAP + 16, D), F32), vm((CAP + 16, 128), F32),
        pltpu.SemaphoreType.DMA((8,)), pltpu.SemaphoreType.DMA((13,)),
    ]
    return call(
        forward_body,
        [SMEM] + [VMEM] * 11 + [ANY] * 6,
        outs,
        scratch,
        (n, x0, cos, sin, kb, kr, *small, *mats),
        flops=2 * 640 * 12e6,
        moved=60 * 2**20,
        name="forward",
    )


def place(keep_ref, send_ref, core, at, pair):
    even = core == 0
    keep_ref[at] = jnp.where(even, pair[0], pair[1]).astype(BF)
    send_ref[at] = jnp.where(even, pair[1], pair[0]).astype(BF)


def feed_back_body(l, k, n_ref, core_ref, g_ref, gains_ref, xs_h, hs_h, fin_h, fout_h, *rest):
    final = k == 1
    out_ref, keep_ref, send_ref, small_ref, x_s, x4_s, h_s, fin, fout, gl_s, a_s, da_s, sem = rest
    core = core_ref[0]
    gain = gains_ref[l, pl.ds(3 if final else 0, 1), :]
    gain4 = gains_ref[l, pl.ds(4, 1), :]

    def run(rows):
        top = pl.ds(0, rows)
        copies = [
            pltpu.make_async_copy(xs_h.at[l, 3 if final else 0, top], x_s.at[top], sem.at[0]),
            pltpu.make_async_copy(hs_h.at[l, k, top], h_s.at[top], sem.at[2]),
            pltpu.make_async_copy(fout_h.at[l, k], fout, sem.at[3]),
            pltpu.make_async_copy(fin_h.at[l, k], fin, sem.at[4]),
        ]
        if final:
            copies.insert(0, pltpu.make_async_copy(xs_h.at[l, 4, top], x4_s.at[top], sem.at[1]))
        for c in copies:
            c.start()
        if final:
            copies[0].wait()
        copies[-4].wait()

        def first(i, at, carry):
            g = g_ref[at, :]
            if final:
                xhat, inv = normalise(x4_s[at, :])
                carry = carry + fold(g * xhat)
                g = norm_back(g, xhat, inv, gain4)
            out_ref[at, :] = g
            gl_s[at, :] = (0.5 * g).astype(BF)
            xhat, _ = normalise(x_s[at, :])
            a_s[at, :] = (xhat * gain).astype(BF)
            da_s[at, :] = jnp.zeros((BLK, D), F32)
            return carry

        gain4_grad = blocks(rows, first, jnp.zeros((8, D), F32))
        for c in copies[-3:]:
            c.wait()

        def chunk(c, carry):
            cols = pl.ds(pl.multiple_of(c * 512, 512), 512)
            h = h_s[top, cols].astype(F32)
            sig = sigmoid(h)
            s = (h * sig).astype(BF)
            ds = dot_nt(gl_s[top, :], fout[cols, :])
            dh = (ds * (sig * (1.0 + h * (1.0 - sig)))).astype(BF)
            dwi = dot_tn(a_s[top, :], dh)
            place(keep_ref, send_ref, core, (c, pl.ds(0, D), slice(None)), (dwi[:, :LANES], dwi[:, LANES:]))
            dwo = dot_tn(gl_s[top, :], s)
            for z in range(4):
                for b in range(2):
                    pair = [
                        dwo[z * 128 + q * 64 : z * 128 + q * 64 + 64, b * LANES : (b + 1) * LANES] for q in range(2)
                    ]
                    at = pl.ds(pl.multiple_of(D + (2 * c + b) * 64, 64), 64)
                    place(keep_ref, send_ref, core, (z, at, slice(None)), pair)
            da_s[top, :] = da_s[top, :] + dot_nt(dh, fin[:, cols])
            return carry

        lax.fori_loop(0, FF // 512, chunk, jnp.int32(0))

        def last(i, at, carry):
            xhat, inv = normalise(x_s[at, :])
            da = da_s[at, :]
            out_ref[at, :] = out_ref[at, :] + norm_back(da, xhat, inv, gain)
            return carry + fold(da * xhat)

        gain_grad = blocks(rows, last, jnp.zeros((8, D), F32))
        small_ref[0:1, :] = total(gain_grad)
        small_ref[1:2, :] = total(gain4_grad)
        if rows < CAP:
            out_ref[pl.ds(rows, CAP - rows), :] = jnp.zeros((CAP - rows, D), F32)

    by_rows(n_ref, run)


def feed_back(l, k, n, core, g, gains, xs, hs, fin, fout):
    vm = pltpu.VMEM
    return call(
        functools.partial(feed_back_body, l, k),
        [SMEM, SMEM, VMEM, VMEM] + [ANY] * 4,
        [
            (struct((CAP, D), F32), VMEM),
            (struct((4, 1024, LANES), BF), VMEM),
            (struct((4, 1024, LANES), BF), VMEM),
            (struct((8, D), F32), VMEM),
        ],
        [
            vm((CAP, D), F32), vm((CAP, D), F32), vm((CAP, FF), BF), vm((D, FF), BF), vm((FF, D), BF),
            vm((CAP, D), BF), vm((CAP, D), BF), vm((CAP, D), F32), pltpu.SemaphoreType.DMA((5,)),
        ],
        (n, core, g, gains, xs, hs, fin, fout),
        flops=8 * 640 * D * FF,
        moved=16 * 2**20,
        name=f"feed_back_{l}_{k}",
    )


def conv_back_body(
    l, n_ref, core_ref, g_ref, kb_ref, gains_ref, taps_ref, mean_ref, var_ref, scale_ref, shift_ref,
    xs_h, u_h, z_h, pin_h, pout_h,
    out_ref, keep_ref, send_ref, small_ref,
    x_s, u_s, z_s, pin, pout, gl_s, a_s, e_s, de_s, gp, dzp, kp, du_s, sem,
):
    core = core_ref[0]
    gain = gains_ref[l, pl.ds(2, 1), :]
    rs = lax.rsqrt(var_ref[pl.ds(l, 1), :] + EPSILON)
    mean = mean_ref[pl.ds(l, 1), :]
    scale = scale_ref[pl.ds(l, 1), :]
    shift = shift_ref[pl.ds(l, 1), :]

    def run(rows):
        top = pl.ds(0, rows)
        copies = [
            pltpu.make_async_copy(pout_h.at[l], pout, sem.at[0]),
            pltpu.make_async_copy(z_h.at[l, top], z_s.at[top], sem.at[1]),
            pltpu.make_async_copy(u_h.at[l, top], u_s.at[top], sem.at[2]),
            pltpu.make_async_copy(xs_h.at[l, 2, top], x_s.at[top], sem.at[3]),
            pltpu.make_async_copy(pin_h.at[l], pin, sem.at[4]),
        ]
        for c in copies:
            c.start()
        for ref, width, value in ((gp, D, 0.0), (dzp, D, 0.0), (kp, 128, -1.0)):
            ref[pl.ds(0, 8), :] = jnp.full((8, width), value, F32)
            ref[pl.ds(rows + 8, 8), :] = jnp.full((8, width), value, F32)

        def low(i, at, carry):
            gl_s[at, :] = g_ref[at, :].astype(BF)
            kp[pl.ds(pl.multiple_of(i * BLK + 8, 8), BLK), :] = kb_ref[at, :]
            return carry

        blocks(rows, low)
        copies[0].wait()
        de_s[top, :] = dot_nt(gl_s[top, :], pout[...])
        for c in copies[1:]:
            c.wait()

        def first(i, at, carry):
            scale_grad, shift_grad = carry
            inner = pl.ds(pl.multiple_of(i * BLK + 8, 8), BLK)
            hat = (z_s[at, :] - mean) * rs
            b = hat * scale + shift
            sig = sigmoid(b)
            e_s[at, :] = (b * sig).astype(BF)
            db = de_s[at, :] * (sig * (1.0 + b * (1.0 - sig)))
            dzp[inner, :] = (db * scale * rs).astype(BF).astype(F32)
            u1 = u_s[at, pl.ds(0, D)].astype(F32)
            u2 = u_s[at, pl.ds(D, D)].astype(F32)
            gp[inner, :] = (u1 * sigmoid(u2)).astype(BF).astype(F32)
            xhat, _ = normalise(x_s[at, :])
            a_s[at, :] = (xhat * gain).astype(BF)
            return (scale_grad + fold(db * hat), shift_grad + fold(db))

        zero = jnp.zeros((8, D), F32)
        scale_grad, shift_grad = blocks(rows, first, (zero, zero))
        small_ref[...] = jnp.zeros(small_ref.shape, F32)
        small_ref[1:2, :] = total(scale_grad)
        small_ref[2:3, :] = total(shift_grad)

        for p in range(PAIRS):
            lanes = slice(p * 128, (p + 1) * 128)

            def taps(t, at, carry, lanes=lanes, p=p):
                wide = pl.ds(pl.multiple_of(t * BLK, BLK), BLK + 16)
                keys = kp[wide, :]
                own = keys[8 : 8 + BLK]
                g = gp[wide, lanes]
                dz = dzp[wide, lanes]
                dz_own = dz[8 : 8 + BLK]
                dg = jnp.zeros((BLK, 128), F32)
                sums = []
                for o in range(KERNEL):
                    mask = keys[4 + o : 4 + o + BLK] == own
                    sums.append(carry[o] + fold(jnp.where(mask, dz_own * g[4 + o : 4 + o + BLK], 0.0)))
                    w = taps_ref[l, KERNEL - 1 - o : KERNEL - o, lanes]
                    dg = dg + jnp.where(mask, w * dz[4 + o : 4 + o + BLK], 0.0)
                u1 = u_s[at, lanes].astype(F32)
                sig = sigmoid(u_s[at, D + p * 128 : D + (p + 1) * 128].astype(F32))
                du_s[at, lanes] = (dg * sig).astype(BF)
                du_s[at, D + p * 128 : D + (p + 1) * 128] = (dg * u1 * sig * (1.0 - sig)).astype(BF)
                return tuple(sums)

            sums = blocks(rows, taps, tuple(jnp.zeros((8, 128), F32) for _ in range(KERNEL)))
            for o in range(KERNEL):
                small_ref[8 + o : 9 + o, lanes] = total(sums[o])

        for z in range(4):
            dwi = dot_tn(a_s[top, :], du_s[top, z * 256 : (z + 1) * 256])
            pair = [
                jnp.concatenate(
                    [dwi[: D // 2, q * 128 : (q + 1) * 128], dwi[D // 2 :, q * 128 : (q + 1) * 128]], axis=1
                )
                for q in range(2)
            ]
            place(keep_ref, send_ref, core, (z, pl.ds(0, 256), slice(None)), pair)
        dwo = dot_tn(gl_s[top, :], e_s[top, :])
        for z in range(4):
            for b in range(2):
                pair = [dwo[z * 128 + q * 64 : z * 128 + q * 64 + 64, b * LANES : (b + 1) * LANES] for q in range(2)]
                place(keep_ref, send_ref, core, (z, pl.ds(256 + b * 64, 64), slice(None)), pair)
        de_s[top, :] = dot_nt(du_s[top, :], pin[...])

        def last(i, at, carry):
            xhat, inv = normalise(x_s[at, :])
            da = de_s[at, :]
            out_ref[at, :] = g_ref[at, :] + norm_back(da, xhat, inv, gain)
            return carry + fold(da * xhat)

        small_ref[0:1, :] = total(blocks(rows, last, zero))

    by_rows(n_ref, run)


def conv_back(l, n, core, g, kb, small, xs, u, z, pin, pout):
    vm = pltpu.VMEM
    return call(
        functools.partial(conv_back_body, l),
        [SMEM, SMEM] + [VMEM] * 8 + [ANY] * 5,
        [
            (struct((CAP, D), F32), VMEM),
            (struct((4, 384, LANES), BF), VMEM),
            (struct((4, 384, LANES), BF), VMEM),
            (struct((24, D), F32), VMEM),
        ],
        [
            vm((CAP, D), F32), vm((CAP, 2 * D), BF), vm((CAP, D), F32), vm((D, 2 * D), BF), vm((D, D), BF),
            vm((CAP, D), BF), vm((CAP, D), BF), vm((CAP, D), BF), vm((CAP, D), F32), vm((CAP + 16, D), F32),
            vm((CAP + 16, D), F32), vm((CAP + 16, 128), F32), vm((CAP, 2 * D), BF), pltpu.SemaphoreType.DMA((5,)),
        ],
        (n, core, g, kb, *small, xs, u, z, pin, pout),
        flops=12 * 640 * D * D,
        moved=12 * 2**20,
        name=f"conv_back_{l}",
    )


def attend_back_body(
    l, n_ref, core_ref, g_ref, cos_ref, sin_ref, gains_ref,
    xs_h, q_h, kv_h, at_h, o_h, ain_h, aout_h,
    out_ref, keep_ref, send_ref, small_ref,
    x_s, q_s, kv_s, at_s, o_s, ain, aout, gl_s, a_s, do_s, dq_s, dkv_s, dp_s, da_s, sem,
):
    core = core_ref[0]
    gain = gains_ref[l, pl.ds(1, 1), :]

    def run(rows):
        tiles = rows // BLK
        top = pl.ds(0, rows)
        wide = pl.ds(0, rows + 2 * BLK)
        copies = [
            pltpu.make_async_copy(aout_h.at[l], aout, sem.at[0]),
            pltpu.make_async_copy(o_h.at[l, top], o_s.at[top], sem.at[1]),
            pltpu.make_async_copy(q_h.at[l, top], q_s.at[top], sem.at[2]),
            pltpu.make_async_copy(kv_h.at[l, wide], kv_s.at[wide], sem.at[3]),
            pltpu.make_async_copy(at_h.at[l, pl.ds(0, tiles)], at_s.at[pl.ds(0, tiles)], sem.at[4]),
            pltpu.make_async_copy(xs_h.at[l, 1, top], x_s.at[top], sem.at[5]),
            pltpu.make_async_copy(ain_h.at[l], ain, sem.at[6]),
        ]
        for c in copies:
            c.start()

        def low(i, at, carry):
            gl_s[at, :] = g_ref[at, :].astype(BF)
            return carry

        blocks(rows, low)

        def clear(i, at, carry):
            dkv_s[at, :] = jnp.zeros((BLK, 2 * D), F32)
            return carry

        blocks(rows + 2 * BLK, clear)
        copies[0].wait()
        do_s[top, :] = dot_nt(gl_s[top, :], aout[...]).astype(BF)
        for c in copies[1:]:
            c.wait()

        def tile(t, at, carry):
            near = pl.ds(pl.multiple_of(t * BLK, BLK), 3 * BLK)
            for p in range(PAIRS):
                lanes = slice(p * 128, (p + 1) * 128)
                vlanes = slice(D + p * 128, D + (p + 1) * 128)
                do = stacked(do_s[at, lanes])
                o = o_s[at, lanes].astype(F32)
                delta = jnp.sum(do.astype(F32) * jnp.concatenate([o, o], axis=0), axis=-1, keepdims=True)
                weights = at_s[t, p]
                da = dot_nt(do, kv_s[near, vlanes])
                ds = (weights.astype(F32) * (da - delta)).astype(BF)
                dq_s[at, lanes] = unstacked(dot_nn(ds, kv_s[near, lanes])) * HD**-0.5
                dkv_s[near, lanes] = dkv_s[near, lanes] + dot_tn(ds, stacked(q_s[at, lanes]))
                dkv_s[near, vlanes] = dkv_s[near, vlanes] + dot_tn(weights, do)
            return carry

        blocks(rows, tile)

        def turn(i, at, carry):
            inner = pl.ds(pl.multiple_of(i * BLK + BLK, BLK), BLK)
            cos, sin = cos_ref[at, :], sin_ref[at, :]
            for p in range(PAIRS):
                lanes = slice(p * 128, (p + 1) * 128)
                dq = dq_s[at, lanes]
                dk = dkv_s[inner, lanes]
                dp_s[at, lanes] = (dq * cos - swap_halves(dq) * sin).astype(BF)
                dp_s[at, D + p * 128 : D + (p + 1) * 128] = (dk * cos - swap_halves(dk) * sin).astype(BF)
                dp_s[at, 2 * D + p * 128 : 2 * D + (p + 1) * 128] = dkv_s[
                    inner, D + p * 128 : D + (p + 1) * 128
                ].astype(BF)
            xhat, _ = normalise(x_s[at, :])
            a_s[at, :] = (xhat * gain).astype(BF)
            return carry

        blocks(rows, turn)

        for z in range(4):
            dwi = dot_tn(dp_s[top, z * 384 : (z + 1) * 384], a_s[top, :])
            for b in range(2):
                pair = [dwi[q * 192 : (q + 1) * 192, b * LANES : (b + 1) * LANES] for q in range(2)]
                place(keep_ref, send_ref, core, (z, pl.ds(b * 192, 192), slice(None)), pair)
        dwo = dot_tn(gl_s[top, :], o_s[top, :])
        for z in range(4):
            for b in range(2):
                pair = [dwo[z * 128 + q * 64 : z * 128 + q * 64 + 64, b * LANES : (b + 1) * LANES] for q in range(2)]
                place(keep_ref, send_ref, core, (z, pl.ds(384 + b * 64, 64), slice(None)), pair)
        da_s[top, :] = dot_nt(dp_s[top, :], ain[...])

        def last(i, at, carry):
            xhat, inv = normalise(x_s[at, :])
            da = da_s[at, :]
            out_ref[at, :] = g_ref[at, :] + norm_back(da, xhat, inv, gain)
            return carry + fold(da * xhat)

        small_ref[0:1, :] = total(blocks(rows, last, jnp.zeros((8, D), F32)))

    by_rows(n_ref, run)


def attend_back(l, n, core, g, cos, sin, gains, xs, q, kv, at, o, ain, aout):
    vm = pltpu.VMEM
    return call(
        functools.partial(attend_back_body, l),
        [SMEM, SMEM] + [VMEM] * 4 + [ANY] * 7,
        [
            (struct((CAP, D), F32), VMEM),
            (struct((4, 512, LANES), BF), VMEM),
            (struct((4, 512, LANES), BF), VMEM),
            (struct((8, D), F32), VMEM),
        ],
        [
            vm((CAP, D), F32), vm((CAP, D), BF), vm((CAP + 2 * BLK, 2 * D), BF),
            vm((CAP // BLK, PAIRS, 2 * BLK, 3 * BLK), BF), vm((CAP, D), BF), vm((D, 3 * D), BF), vm((D, D), BF),
            vm((CAP, D), BF), vm((CAP, D), BF), vm((CAP, D), BF), vm((CAP, D), F32),
            vm((CAP + 2 * BLK, 2 * D), F32), vm((CAP, 3 * D), BF), vm((CAP, D), F32), pltpu.SemaphoreType.DMA((7,)),
        ],
        (n, core, g, cos, sin, gains, xs, q, kv, at, o, ain, aout),
        flops=16 * 640 * D * D,
        moved=20 * 2**20,
        name=f"attend_back_{l}",
    )


def add(*terms):
    acc = terms[0].astype(F32)
    for term in terms[1:]:
        acc = acc + term.astype(F32)
    return acc.astype(BF)


def split_xy_body(sizes, place_ref, *refs):
    count = len(sizes)
    keeps, gots = refs[:count], refs[count : 2 * count]
    a_keep, a_send, b_keep, b_send = refs[2 * count :]
    x, y = place_ref[0], place_ref[1]
    off = 0
    for keep, got, n in zip(keeps, gots, sizes):
        at = pl.ds(off, n)

        def one(z, carry, keep=keep, got=got, at=at):
            for j in range(2):
                a_keep[z, j, at] = add(keep[z, 0, j, x], got[z, 0, j, x])
                a_send[z, j, at] = add(keep[z, 0, j, 1 - x], got[z, 0, j, 1 - x])
                b_keep[z, j, at] = add(keep[z, 1, y, j], got[z, 1, y, j])
                b_send[z, j, at] = add(keep[z, 1, 1 - y, j], got[z, 1, 1 - y, j])
            return carry

        lax.fori_loop(0, 4, one, jnp.int32(0))
        off += n


def split_yx_body(place_ref, a_keep, a_got, b_keep, b_got, a2_keep, a2_send, b2_keep, b2_send):
    x, y = place_ref[0], place_ref[1]

    def one(z, carry):
        a2_keep[z] = add(a_keep[z, y], a_got[z, y])
        a2_send[z] = add(a_keep[z, 1 - y], a_got[z, 1 - y])
        b2_keep[z] = add(b_keep[z, x], b_got[z, x])
        b2_send[z] = add(b_keep[z, 1 - x], b_got[z, 1 - x])
        return carry

    lax.fori_loop(0, 4, one, jnp.int32(0))


def split_z_body(place_ref, a_keep, a_got, b_keep, b_got, own, one, two, three):
    z = place_ref[2]
    for k, ref in enumerate((own, one, two, three)):
        at = lax.rem(z + k, 4)
        ref[0] = add(a_keep[at], a_got[at])
        ref[1] = add(b_keep[at], b_got[at])


def sum_four_body(a, b, c, d, out):
    out[...] = add(a[...], b[...], c[...], d[...])


def row_pairs(bit):
    return [(i, i ^ bit) for i in range(4)]


def summed_group(spot, keeps, sends):
    core_pairs = [(i, i ^ 1) for i in range(8)]
    gots = [lax.ppermute(s, "tm", core_pairs) for s in sends]
    sizes = [k.shape[1] // 8 for k in keeps]
    n = sum(sizes)
    shaped = lambda v: v.reshape(4, 2, 2, 2, v.shape[1] // 8, LANES)
    quarter = struct((4, 2, n, LANES), BF)
    moved = 6 * 4 * 2 * n * LANES * 2
    a_keep, a_send, b_keep, b_send = call(
        functools.partial(split_xy_body, sizes),
        [SMEM] + [VMEM] * (2 * len(sizes)),
        [(quarter, VMEM)] * 4,
        [],
        (spot, *map(shaped, keeps), *map(shaped, gots)),
        moved=2 * moved,
        name="split_xy",
    )
    a_got = lax.ppermute(a_send, "rows", row_pairs(1))
    b_got = lax.ppermute(b_send, "rows", row_pairs(2))
    eighth = struct((4, n, LANES), BF)
    a_keep, a_send, b_keep, b_send = call(
        split_yx_body,
        [SMEM] + [VMEM] * 4,
        [(eighth, VMEM)] * 4,
        [],
        (spot, a_keep, a_got, b_keep, b_got),
        moved=moved,
        name="split_yx",
    )
    a_got = lax.ppermute(a_send, "rows", row_pairs(2))
    b_got = lax.ppermute(b_send, "rows", row_pairs(1))
    piece = struct((2, n, LANES), BF)
    own, *others = call(
        split_z_body,
        [SMEM] + [VMEM] * 4,
        [(piece, VMEM)] * 4,
        [],
        (spot, a_keep, a_got, b_keep, b_got),
        moved=moved // 2,
        name="split_z",
    )
    gots = [
        lax.ppermute(v, "tm", [(i, (i + 2 * k) % 8) for i in range(8)]) for k, v in zip((1, 2, 3), others)
    ]
    mine = call(
        sum_four_body,
        [VMEM] * 4,
        [(piece, VMEM)],
        [],
        (own, *gots),
        moved=moved // 4,
        name="sum_four",
    )[0]
    others = [lax.ppermute(mine, "rows", row_pairs(bit)) for bit in (1, 2, 3)]
    me = 2 * spot[1] + spot[0]
    by_bit = jnp.stack([mine, *others])
    by_owner = jnp.stack([lax.dynamic_index_in_dim(by_bit, jnp.bitwise_xor(me, r), 0, False) for r in range(4)])
    whole = jnp.swapaxes(by_owner, 0, 1)
    out = []
    off = 0
    for size in sizes:
        out.append(whole[:, :, off : off + size].reshape(8 * size, LANES))
        off += size
    return out


def rows_of(chunk, blocks_of):
    r = chunk.shape[0] // blocks_of
    return jnp.swapaxes(chunk.reshape(blocks_of, r, LANES), 0, 1).reshape(r, blocks_of * LANES)


def feed_parts(chunk):
    return chunk[:D], rows_of(chunk[D:], FF // LANES).T


def conv_parts(chunk):
    point_in = jnp.concatenate([chunk[:256, :128], chunk[:256, 128:]], axis=0)
    return point_in, rows_of(chunk[256:], 2).T


def attend_parts(chunk):
    return rows_of(chunk[:384], 2).T, rows_of(chunk[384:], 2).T


def per_device(
    frames, segment_ids, norm_gains, feed_in, feed_out, attend_in, attend_out, point_in, depthwise, stat_mean,
    stat_var, batch_scale, batch_shift, point_out, cotangent,
):
    batches, row_count, frame_count, model_dim = frames.shape
    layers = norm_gains.shape[0]
    tm_size = lax.axis_size("tm")
    rows_size = lax.axis_size("rows")
    tm = lax.axis_index("tm")
    row = lax.axis_index("rows")
    fast = tm_size == 8 and rows_size == 4
    half = batches // 2

    ids = segment_ids[:, 0] + 1
    below = shifted(ids, "tm", 1)
    above = shifted(ids, "tm", -1)

    def windows(own):
        pairs = own.reshape((half, 2) + own.shape[1:])
        from_above = shifted(pairs[:, 0], "tm", -1)
        from_below = shifted(pairs[:, 1], "tm", 1)
        even = jnp.concatenate([pairs[:, 0], from_above], axis=1)
        odd = jnp.concatenate([from_below, pairs[:, 1]], axis=1)
        return jnp.stack([even, odd], axis=1).reshape((batches * 2 * frame_count,) + own.shape[2:])

    pair_ids = ids.reshape(half, 2, frame_count)
    pair_below = below.reshape(half, 2, frame_count)
    pair_above = above.reshape(half, 2, frame_count)
    even_keep = jnp.concatenate(
        [pair_ids[:, 0] != pair_below[:, 0, -1:], pair_above[:, 0] == pair_ids[:, 0, -1:]], axis=1
    )
    odd_keep = jnp.concatenate(
        [pair_below[:, 1] == pair_ids[:, 1, :1], pair_ids[:, 1] != pair_above[:, 1, :1]], axis=1
    )
    even_ids = jnp.concatenate([pair_ids[:, 0], pair_above[:, 0]], axis=1)
    odd_ids = jnp.concatenate([pair_below[:, 1], pair_ids[:, 1]], axis=1)
    keep = jnp.stack([even_keep, odd_keep], axis=1).reshape(-1)
    win_ids = jnp.stack([even_ids, odd_ids], axis=1).reshape(batches, 2 * frame_count)
    key = (win_ids + 4096 * jnp.arange(batches, dtype=jnp.int32)[:, None]).reshape(-1).astype(F32)
    n = jnp.sum(keep.astype(jnp.int32)).reshape(1)

    x0, chooser, cos, sin, kb, kr = pack(keep.astype(F32), key, windows(frames[:, 0]))
    small = (norm_gains, depthwise, stat_mean, stat_var, batch_scale, batch_shift)
    mats = (feed_in, feed_out, attend_in, attend_out, point_in, point_out)
    act, xs, hs, q, kv, at, o, u, z = forward(n, x0, cos, sin, kb, kr, small, mats)

    def unpacked(packed):
        spread = lax.dot_general(
            chooser, packed, (((0,), (0,)), ((), ())), preferred_element_type=F32
        ).astype(BF).reshape(half, 2, 2, frame_count, model_dim)
        from_below = shifted(spread[:, 0, 1], "tm", 1)
        from_above = shifted(spread[:, 1, 0], "tm", -1)
        even = spread[:, 0, 0] + from_below
        odd = spread[:, 1, 1] + from_above
        return jnp.stack([even, odd], axis=1).reshape(batches, 1, frame_count, model_dim)

    activations = unpacked(act)
    g = jnp.dot(chooser, windows(cotangent[:, 0]), preferred_element_type=F32)

    if fast:
        spot = jnp.stack([row % 2, row // 2, tm // 2]).astype(jnp.int32)
        core = (tm % 2).astype(jnp.int32).reshape(1)
    else:
        spot = None
        core = jnp.zeros((1,), jnp.int32)

    members = {}
    smalls = {}
    for l in reversed(range(layers)):
        g, keep_b, send_b, smalls[l, "f1"] = feed_back(l, 1, n, core, g, norm_gains, xs, hs, feed_in, feed_out)
        members[l, "f1"] = (keep_b, send_b)
        g, keep_b, send_b, smalls[l, "c"] = conv_back(l, n, core, g, kb, small, xs, u, z, point_in, point_out)
        members[l, "c"] = (keep_b, send_b)
        g, keep_b, send_b, smalls[l, "a"] = attend_back(
            l, n, core, g, cos, sin, norm_gains, xs, q, kv, at, o, attend_in, attend_out
        )
        members[l, "a"] = (keep_b, send_b)
        g, keep_b, send_b, smalls[l, "f0"] = feed_back(l, 0, n, core, g, norm_gains, xs, hs, feed_in, feed_out)
        members[l, "f0"] = (keep_b, send_b)
    frames_grad = unpacked(g.astype(BF))

    small_rows = []
    for l in range(layers):
        f0, a, c, f1 = (smalls[l, name] for name in ("f0", "a", "c", "f1"))
        small_rows += [f0[0:1], a[0:1], c[0:1], f1[0:1], f1[1:2], c[8 : 8 + KERNEL], c[1:3]]
    per_layer = 5 + KERNEL + 2
    small_all = jnp.concatenate(small_rows, axis=0)

    if fast:
        chunks = small_all.reshape(layers * per_layer, 4, 2, D // 8)
        chunks = jnp.moveaxis(chunks, 0, 2).reshape(4, 2, -1, LANES)
        chunks = jnp.pad(chunks, ((0, 0), (0, 0), (0, 128 - chunks.shape[2]), (0, 0))).astype(BF)
        members["small"] = (
            lax.dynamic_index_in_dim(chunks, core[0], 1, False),
            lax.dynamic_index_in_dim(chunks, 1 - core[0], 1, False),
        )
        groups = []
        for l in reversed(range(layers)):
            groups.append([(l, "f1"), (l, "c"), (l, "a")])
            groups.append([(l, "f0")] + (["small"] if l == 0 else []))
        done = {}
        for names in groups:
            parts = summed_group(spot, [members[m][0] for m in names], [members[m][1] for m in names])
            done.update(zip(names, parts))
        pick = lambda name, split: [split(done[l, name]) for l in range(layers)]
        f0, a, c, f1 = (
            pick("f0", feed_parts), pick("a", attend_parts), pick("c", conv_parts), pick("f1", feed_parts)
        )
        fin = jnp.stack([jnp.stack([f0[l][0], f1[l][0]]) for l in range(layers)])
        fout = jnp.stack([jnp.stack([f0[l][1], f1[l][1]]) for l in range(layers)])
        ain, aout = (jnp.stack([a[l][i] for l in range(layers)]) for i in range(2))
        pin, pout = (jnp.stack([c[l][i] for l in range(layers)]) for i in range(2))
        mats_out = [v.astype(F32) for v in (fin, fout, ain, aout, pin, pout)]
        lines = layers * per_layer * (D // 8) // LANES
        small_out = done["small"][:lines].reshape(layers, per_layer, D // 8).astype(F32)
    else:
        def natural(name, l):
            even, odd = members[l, name]
            return jnp.stack([even, odd], axis=1).astype(F32).reshape(8, -1, LANES)

        def wide(v, count):
            r = v.shape[1] // count
            return jnp.swapaxes(v.reshape(8, count, r, LANES), 1, 2).reshape(8 * r, count * LANES)

        def over_all(v, dim):
            v = lax.psum_scatter(v, "tm", scatter_dimension=dim, tiled=True)
            return lax.psum(v, "rows")

        fin, fout, ain, aout, pin, pout = [], [], [], [], [], []
        for l in range(layers):
            f = [natural("f0", l), natural("f1", l)]
            fin.append(jnp.stack([jnp.moveaxis(v[:, :D], 0, 1).reshape(D, FF) for v in f]))
            fout.append(jnp.stack([wide(v[:, D:], FF // LANES).T for v in f]))
            v = natural("a", l)
            ain.append(wide(v[:, :384], 2).T)
            aout.append(wide(v[:, 384:], 2).T)
            v = natural("c", l)
            top = jnp.concatenate([v[:, :256, :128], v[:, :256, 128:]], axis=1)
            pin.append(jnp.moveaxis(top, 0, 1).reshape(D, 2 * D))
            pout.append(wide(v[:, 256:], 2).T)
        mats_out = [over_all(jnp.stack(v), jnp.stack(v).ndim - 1) for v in (fin, fout, ain, aout, pin, pout)]
        small_out = over_all(small_all, 1).reshape(layers, per_layer, -1)

    fin, fout, ain, aout, pin, pout = mats_out
    return (
        activations,
        frames_grad,
        small_out[:, :5],
        fin,
        fout,
        ain,
        aout,
        pin,
        small_out[:, 5 : 5 + KERNEL],
        small_out[:, 5 + KERNEL],
        small_out[:, 6 + KERNEL],
        pout,
    )


def solution(mesh):
    rep = P()
    in_specs = (
        P(None, "rows", "tm", None), P(None, "rows", "tm"), rep, rep, rep, rep, rep, rep, rep, rep, rep, rep, rep, rep,
        P(None, "rows", "tm", None),
    )
    out_specs = (
        P(None, "rows", "tm", None), P(None, "rows", "tm", None), P(None, None, "tm"), P(None, None, None, "tm"),
        P(None, None, None, "tm"), P(None, None, "tm"), P(None, None, "tm"), P(None, None, "tm"),
        P(None, None, "tm"), P(None, "tm"), P(None, "tm"), P(None, None, "tm"),
    )
    return jax.shard_map(per_device, mesh=mesh, in_specs=in_specs, out_specs=out_specs, check_vma=False)
```

time: 1970 us -> 531 us (0.27)
  blocking collectives: 583 us -> 0 us
  local copies, waits for them, and re-layouts: 565 us -> 22.9 us
  matrix products: 307 us -> 8.47 us
  Pallas kernels: 0 us -> 284 us
  other arithmetic: 182 us -> 15.3 us
  starting transfers between devices: 185 us -> 80.4 us
  between operations: 32.5 us -> 2.16 us
    unnamed x1 -> x0, blocking collectives: 530 us -> none
    unnamed x2215 -> x86, local copies, waits for them, and re-layouts: 484 us -> 9.29 us
    dot_general x240 -> x3, matrix products: 307 us -> 8.47 us  [the longest x2 4.3 us: unpacked(): lax.dot_general(chooser, packed, (((0,), (0,)), ((), ())), preferred_elem...]
    pallas_call x0 -> x26, Pallas kernels: none -> 284 us  [call(): pl.pallas_call(body, out_shape=[s for s, _ in outs], in_specs=ins, out_sp...]
    ppermute x50 -> x49, waiting for transfers between devices: 17.7 us -> 102 us  [the longest x12 33.4 us: summed_group(): others = [lax.ppermute(mine, 'rows', row_pairs(bit)) for bit in (1, 2, 3)]]
    ppermute x50 -> x49, starting transfers between devices: 138 us -> 55.8 us  [the longest x12 22.5 us: summed_group(): lax.ppermute(v, 'tm', [(i, (i + 2 * k) % 8) for i in range(8)])]
    add x51 -> x2, other arithmetic: 72.2 us -> 0.7 us  [the longest x1 0.7 us: per_device(): ids = segment_ids[:, 0] + 1]
    another operation x31 -> x5, local copies, waits for them, and re-layouts: 44.4 us -> 1.74 us  [the longest x2 1.66 us: unpacked(): jnp.stack([even, odd], axis=1).reshape(batches, 1, frame_count, model_dim)]
  transfers between devices with their start and end apart: 80 -> 59, of which waited for: 20 -> 17; matrix products, arithmetic and copies ran while one was open for 37% -> 5% of each run, Pallas kernels for 0% -> 10%
where the time goes in v1:
time: 531 us; the launch traced here: 522 us
  Pallas kernels  284 us (53%)
  waiting for transfers between devices  109 us (21%)
  starting transfers between devices  80.4 us (15%)
  local copies, waits for them, and re-layouts  22.9 us (4%)
  other arithmetic  15.3 us (3%)
  matrix products  8.47 us (2%)
    pallas_call x26, Pallas kernels, call(): pl.pallas_call(body, out_shape=[s for s, _ in outs], in_specs=ins, out_sp...  284 us
    ppermute x12, waiting for transfers between devices, summed_group(): others = [lax.ppermute(mine, 'rows', row_pairs(bit)) for bit in (1, 2, 3)]  33.4 us
    ppermute x12, waiting for transfers between devices, summed_group(): lax.ppermute(v, 'tm', [(i, (i + 2 * k) % 8) for i in range(8)])  29.7 us
    ppermute x4, waiting for transfers between devices, summed_group(): a_got = lax.ppermute(a_send, 'rows', row_pairs(1))  29.6 us
    ppermute x10, starting transfers between devices, shifted(): return lax.ppermute(array, axis, pairs)  24.6 us
    ppermute x12, starting transfers between devices, summed_group(): lax.ppermute(v, 'tm', [(i, (i + 2 * k) % 8) for i in range(8)])  22.5 us
    ppermute x12, starting transfers between devices, summed_group(): others = [lax.ppermute(mine, 'rows', row_pairs(bit)) for bit in (1, 2, 3)]  13.5 us
  transfers between devices with their start and end apart: 59, of which 17 were waited for; matrix products, arithmetic and copies ran while one was open for 5% of the time, Pallas kernels for 10%

profile of v1, /device:TPU:10, one launch (start us, length us, event | category | flops | bytes accessed | tf_op | source)
XLA Modules:
  0.0 522.1 jit_solution(8912744904766595494)
XLA Ops:
  12.9 3.6 collective-permute-start.6
  27.3 7.1 %pack.1 = (f32[1024,512]{1,0:T(8,128)}, bf16[1024,1024]{1,0:T(8,128)(2,1)}, f32[1024,128]{1,0:T(8,128)}, f32[1024,128]{1,0:T(8,128)}, f32[1024,128]{1,0:T(8,128)}, /*index=5*/f32[8,1280]{1,0:T(8,128)}) custom-call(f32[1,1024]{1,0:T(1,128)} %reshape.348.keep_ref, f32[1,1024]{1,0:T(1,128)} %add_convert_fusion.key_ref, ...), custom_call_target="tpu_custom_call" | custom-call | flops 1073741824 | bytes 8388608 | tf_op jit(solution)/shard_map/pack/pallas_call | solution.py:42
  34.4 4.2 fusion.20.g_ref
  38.6 64.2 %forward.1 = (bf16[1024,512]{1,0:T(8,128)(2,1)}, f32[2,5,1024,512]{3,2,1,0:T(8,128)}, bf16[2,2,1024,2048]{3,2,1,0:T(8,128)(2,1)}, bf16[2,1024,512]{2,1,0:T(8,128...) custom-call(s32[1]{0:T(128)} %bitcast.21.n_ref, ...), custom_call_target="tpu_custom_call" | custom-call | flops 15360000000 | bytes 62914560 | tf_op jit(solution)/shard_map/forward/pallas_call | solution.py:42
  102.8 18.2 %feed_back_1_1.1 = (f32[1024,512]{1,0:T(8,128)}, bf16[4,1024,256]{2,1,0:T(8,128)(2,1)}, bf16[4,1024,256]{2,1,0:T(8,128)(2,1)}, f32[8,512]{1,0:T(8,128)}) custom-call(s32[1]{0:T(128)} %bitcast.21.n_ref, s32[1]{0:T(128)} %bitcast.30.core_ref, f32[1024,512]{1,0:T(8,128)} %fusion.20.g_ref, f32[2,5,512]{2,1,0:T(8,128)} %copy.184.gains_ref, ...), custom_call_target="tpu_custom_call" | custom-call | flops 5368709120 | bytes 16777216 | tf_op jit(solution)/shard_map/feed_back_1_1/pallas_call | solution.py:42
  120.9 21.8 %conv_back_1.1 = (f32[1024,512]{1,0:T(8,128)}, bf16[4,384,256]{2,1,0:T(8,128)(2,1)}, bf16[4,384,256]{2,1,0:T(8,128)(2,1)}, f32[24,512]{1,0:T(8,128)}) custom-call(s32[1]{0:T(128)} %bitcast.21.n_ref, s32[1]{0:T(128)} %bitcast.30.core_ref, f32[1024,512]{1,0:T(8,128)} %get-tuple-element.116.g_ref, f32[1024,128]{1,0:T(8,128)} %get-tuple-element.111.kb_ref, ...), custom_call_target="tpu_custom_call" | custom-call | flops 2013265920 | bytes 12582912 | tf_op jit(solution)/shard_map/conv_back_1/pallas_call | solution.py:42
  142.8 23.4 %attend_back_1.1 = (f32[1024,512]{1,0:T(8,128)}, bf16[4,512,256]{2,1,0:T(8,128)(2,1)}, bf16[4,512,256]{2,1,0:T(8,128)(2,1)}, f32[8,512]{1,0:T(8,128)}) custom-call(s32[1]{0:T(128)} %bitcast.21.n_ref, s32[1]{0:T(128)} %bitcast.30.core_ref, f32[1024,512]{1,0:T(8,128)} %get-tuple-element.119.g_ref, f32[1024,128]{1,0:T(8,128)} %get-tuple-element.109.cos_ref, ...), custom_call_target="tpu_custom_call" | custom-call | flops 2684354560 | bytes 20971520 | tf_op jit(solution)/shard_map/attend_back_1/pallas_call | solution.py:42
  166.2 17.2 %feed_back_1_0.1 = (f32[1024,512]{1,0:T(8,128)}, bf16[4,1024,256]{2,1,0:T(8,128)(2,1)}, bf16[4,1024,256]{2,1,0:T(8,128)(2,1)}, f32[8,512]{1,0:T(8,128)}) custom-call(s32[1]{0:T(128)} %bitcast.21.n_ref, s32[1]{0:T(128)} %bitcast.30.core_ref, f32[1024,512]{1,0:T(8,128)} %get-tuple-element.124.g_ref, f32[2,5,512]{2,1,0:T(8,128)} %copy.184.gains_ref, ...), custom_call_target="tpu_custom_call" | custom-call | flops 5368709120 | bytes 16777216 | tf_op jit(solution)/shard_map/feed_back_1_0/pallas_call | solution.py:42
  183.5 18.1 %feed_back_0_1.1 = (f32[1024,512]{1,0:T(8,128)}, bf16[4,1024,256]{2,1,0:T(8,128)(2,1)}, bf16[4,1024,256]{2,1,0:T(8,128)(2,1)}, f32[8,512]{1,0:T(8,128)}) custom-call(s32[1]{0:T(128)} %bitcast.21.n_ref, s32[1]{0:T(128)} %bitcast.30.core_ref, f32[1024,512]{1,0:T(8,128)} %get-tuple-element.125.g_ref, f32[2,5,512]{2,1,0:T(8,128)} %copy.184.gains_ref, ...), custom_call_target="tpu_custom_call" | custom-call | flops 5368709120 | bytes 16777216 | tf_op jit(solution)/shard_map/feed_back_0_1/pallas_call | solution.py:42
  201.6 21.8 %conv_back_0.1 = (f32[1024,512]{1,0:T(8,128)}, bf16[4,384,256]{2,1,0:T(8,128)(2,1)}, bf16[4,384,256]{2,1,0:T(8,128)(2,1)}, f32[24,512]{1,0:T(8,128)}) custom-call(s32[1]{0:T(128)} %bitcast.21.n_ref, s32[1]{0:T(128)} %bitcast.30.core_ref, f32[1024,512]{1,0:T(8,128)} %get-tuple-element.126.g_ref, f32[1024,128]{1,0:T(8,128)} %get-tuple-element.111.kb_ref, ...), custom_call_target="tpu_custom_call" | custom-call | flops 2013265920 | bytes 12582912 | tf_op jit(solution)/shard_map/conv_back_0/pallas_call | solution.py:42
  223.4 23.4 %attend_back_0.1 = (f32[1024,512]{1,0:T(8,128)}, bf16[4,512,256]{2,1,0:T(8,128)(2,1)}, bf16[4,512,256]{2,1,0:T(8,128)(2,1)}, f32[8,512]{1,0:T(8,128)}) custom-call(s32[1]{0:T(128)} %bitcast.21.n_ref, s32[1]{0:T(128)} %bitcast.30.core_ref, f32[1024,512]{1,0:T(8,128)} %get-tuple-element.127.g_ref, f32[1024,128]{1,0:T(8,128)} %get-tuple-element.109.cos_ref, ...), custom_call_target="tpu_custom_call" | custom-call | flops 2684354560 | bytes 20971520 | tf_op jit(solution)/shard_map/attend_back_0/pallas_call | solution.py:42
  246.8 17.5 %feed_back_0_0.1 = (f32[1024,512]{1,0:T(8,128)}, bf16[4,1024,256]{2,1,0:T(8,128)(2,1)}, bf16[4,1024,256]{2,1,0:T(8,128)(2,1)}, f32[8,512]{1,0:T(8,128)}) custom-call(s32[1]{0:T(128)} %bitcast.21.n_ref, s32[1]{0:T(128)} %bitcast.30.core_ref, f32[1024,512]{1,0:T(8,128)} %get-tuple-element.128.g_ref, f32[2,5,512]{2,1,0:T(8,128)} %copy.184.gains_ref, ...), custom_call_target="tpu_custom_call" | custom-call | flops 5368709120 | bytes 16777216 | tf_op jit(solution)/shard_map/feed_back_0_0/pallas_call | solution.py:42
  270.8 3.8 collective-permute-start.5
  287.4 4.0 collective-permute-done.8
  293.5 4.3 split_xy.4
  298.3 4.0 split_xy.6
  305.4 18.9 %collective-permute-done.36.a_got = bf16[4,2,128,256]{3,2,1,0:T(8,128)(2,1)S(1)} collective-permute-done((bf16[4,2,128,256]{3,2,1,0:T(8,128)(2,1)}, bf16[4,2,128,256]{3,2,1,0:T(8,128)(2,1)S(1)}, u32[]{:S(2)}, u32[]{:S(2)}) %collective-permute-start.36) | collective-permute-done | bytes 524320 | tf_op jit(solution)/shard_map/ppermute | solution.py:896
  330.0 9.8 %collective-permute-done.37.b_got = bf16[4,2,128,256]{3,2,1,0:T(8,128)(2,1)} collective-permute-done((bf16[4,2,128,256]{3,2,1,0:T(8,128)(2,1)}, bf16[4,2,128,256]{3,2,1,0:T(8,128)(2,1)}, u32[]{:S(2)}, u32[]{:S(2)}) %collective-permute-start.37) | collective-permute-done | bytes 524320 | tf_op jit(solution)/shard_map/ppermute | solution.py:897
  348.7 6.1 %split_xy.7 = (bf16[4,2,240,256]{3,2,1,0:T(8,128)(2,1)}, bf16[4,2,240,256]{3,2,1,0:T(8,128)(2,1)}, bf16[4,2,240,256]{3,2,1,0:T(8,128)(2,1)}, bf16[4,2,240,256]{3,2,1,0:T(8,128)(2,1)}) custom-call(s32[3]{0:T(128)} %pad_add_fusion.3.place_ref, bf16[4,2,2,2,128,256]{5,4,3,2,1,0:T(8,128)(2,1)} %bitcast.291, bf16[4,2,2,2,48,256]{5,4,3,2,1,0:T(8,128)(2,1)} %bitcast.330, ...), custom_call_target="tpu_custom_call" | custom-call | bytes 11796480 | tf_op jit(solution)/shard_map/split_xy/pallas_call | solution.py:42
  354.8 6.3 %split_xy.5 = (bf16[4,2,240,256]{3,2,1,0:T(8,128)(2,1)}, bf16[4,2,240,256]{3,2,1,0:T(8,128)(2,1)}, bf16[4,2,240,256]{3,2,1,0:T(8,128)(2,1)}, bf16[4,2,240,256]{3,2,1,0:T(8,128)(2,1)}) custom-call(s32[3]{0:T(128)} %pad_add_fusion.3.place_ref, bf16[4,2,2,2,128,256]{5,4,3,2,1,0:T(8,128)(2,1)} %bitcast.292, bf16[4,2,2,2,48,256]{5,4,3,2,1,0:T(8,128)(2,1)} %bitcast.331, ...), custom_call_target="tpu_custom_call" | custom-call | bytes 11796480 | tf_op jit(solution)/shard_map/split_xy/pallas_call | solution.py:42
  368.9 3.6 collective-permute-done.40.b
  375.1 4.1 collective-permute-done.41.c
  389.3 3.8 collective-permute-start.17
  395.1 10.7 %collective-permute-done.25.a_got = bf16[4,2,240,256]{3,2,1,0:T(8,128)(2,1)} collective-permute-done((bf16[4,2,240,256]{3,2,1,0:T(8,128)(2,1)}, bf16[4,2,240,256]{3,2,1,0:T(8,128)(2,1)}, u32[]{:S(2)}, u32[]{:S(2)}) %collective-permute-start.25) | collective-permute-done | bytes 983072 | tf_op jit(solution)/shard_map/ppermute | solution.py:896
  411.1 3.8 split_yx.7
  414.9 4.0 split_yx.5
  426.5 8.1 %collective-permute-done.21 = bf16[2,144,256]{2,1,0:T(8,128)(2,1)S(1)} collective-permute-done((bf16[2,144,256]{2,1,0:T(8,128)(2,1)}, bf16[2,144,256]{2,1,0:T(8,128)(2,1)S(1)}, u32[]{:S(2)}, u32[]{:S(2)}) %collective-permute-start.21) | collective-permute-done | bytes 147488 | tf_op jit(solution)/shard_map/ppermute | solution.py:932
  435.2 11.9 %collective-permute-done.20 = bf16[2,144,256]{2,1,0:T(8,128)(2,1)S(1)} collective-permute-done((bf16[2,144,256]{2,1,0:T(8,128)(2,1)}, bf16[2,144,256]{2,1,0:T(8,128)(2,1)S(1)}, u32[]{:S(2)}, u32[]{:S(2)}) %collective-permute-start.20) | collective-permute-done | bytes 147488 | tf_op jit(solution)/shard_map/ppermute | solution.py:932
  447.6 4.5 collective-permute-done.19
  469.5 18.4 %collective-permute-done.54.c = bf16[2,240,256]{2,1,0:T(8,128)(2,1)S(1)} collective-permute-done((bf16[2,240,256]{2,1,0:T(8,128)(2,1)}, bf16[2,240,256]{2,1,0:T(8,128)(2,1)S(1)}, u32[]{:S(2)}, u32[]{:S(2)}) %collective-permute-start.54) | collective-permute-done | bytes 245792 | tf_op jit(solution)/shard_map/ppermute | solution.py:921
  505.7 5.0 collective-permute-done.34
  510.7 3.8 collective-permute-done.33
  (326 shorter events, 140.6 us)
Async XLA Ops:
  6.8 19.3 %collective-permute-start.2 = (bf16[2,128,512]{2,1,0:T(8,128)(2,1)S(1)}, bf16[2,128,512]{2,1,0:T(8,128)(2,1)S(1)}, u32[]{:S(2)}, u32[]{:S(2)}) collective-permute-start(bf16[2,128,512]{2,1,0:T(8,128)(2,1)S(1)} %get-tuple-element.272), channel_id=1, source_target_pairs={{1,0},{2,1},{3,2},{4,3},{5,4},{6,5},{7,6},{9,8},{10,9},{11,10},{12... | collective-permute-start | bytes 786440 | tf_op jit(solution)/shard_map/ppermute | solution.py:34
  264.3 27.1 %collective-permute-start.10 = (bf16[4,1024,256]{2,1,0:T(8,128)(2,1)}, bf16[4,1024,256]{2,1,0:T(8,128)(2,1)S(1)}, u32[]{:S(2)}, u32[]{:S(2)}) collective-permute-start(bf16[4,1024,256]{2,1,0:T(8,128)(2,1)} %get-tuple-element.139), channel_id=1, source_target_pairs={{0,1},{1,0},{2,3},{3,2},{4,5},{5,4},{6,7},{7,6},{8,9},{9,8},{10,11... | collective-permute-start | bytes 6291464 | tf_op jit(solution)/shard_map/ppermute | solution.py:881
  264.4 33.4 %collective-permute-start.35 = (bf16[4,1024,256]{2,1,0:T(8,128)(2,1)}, bf16[4,1024,256]{2,1,0:T(8,128)(2,1)}, u32[]{:S(2)}, u32[]{:S(2)}) collective-permute-start(bf16[4,1024,256]{2,1,0:T(8,128)(2,1)} %get-tuple-element.171), channel_id=1, source_target_pairs={{0,1},{1,0},{2,3},{3,2},{4,5},{5,4},{6,7},{7,6},{8,9},{9,8},{10,11... | collective-permute-start | bytes 6291464 | tf_op jit(solution)/shard_map/ppermute | solution.py:881
  274.6 27.7 %collective-permute-start.47 = (bf16[4,384,256]{2,1,0:T(8,128)(2,1)}, bf16[4,384,256]{2,1,0:T(8,128)(2,1)}, u32[]{:S(2)}, u32[]{:S(2)}) collective-permute-start(bf16[4,384,256]{2,1,0:T(8,128)(2,1)} %get-tuple-element.188), channel_id=1, source_target_pairs={{0,1},{1,0},{2,3},{3,2},{4,5},{5,4},{6,7},{7,6},{8,9},{9,8},{10,11... | collective-permute-start | bytes 2359304 | tf_op jit(solution)/shard_map/ppermute | solution.py:881
  285.7 60.9 %collective-permute-start.46 = (bf16[4,1024,256]{2,1,0:T(8,128)(2,1)}, bf16[4,1024,256]{2,1,0:T(8,128)(2,1)}, u32[]{:S(2)}, u32[]{:S(2)}) collective-permute-start(bf16[4,1024,256]{2,1,0:T(8,128)(2,1)} %get-tuple-element.187), channel_id=1, source_target_pairs={{0,1},{1,0},{2,3},{3,2},{4,5},{5,4},{6,7},{7,6},{8,9},{9,8},{10,11... | collective-permute-start | bytes 6291464 | tf_op jit(solution)/shard_map/ppermute | solution.py:881
  292.1 55.0 %collective-permute-start.22 = (bf16[4,1024,256]{2,1,0:T(8,128)(2,1)}, bf16[4,1024,256]{2,1,0:T(8,128)(2,1)}, u32[]{:S(2)}, u32[]{:S(2)}) collective-permute-start(bf16[4,1024,256]{2,1,0:T(8,128)(2,1)} %get-tuple-element.155), channel_id=1, source_target_pairs={{0,1},{1,0},{2,3},{3,2},{4,5},{5,4},{6,7},{7,6},{8,9},{9,8},{10,11... | collective-permute-start | bytes 6291464 | tf_op jit(solution)/shard_map/ppermute | solution.py:881
  297.8 26.5 %collective-permute-start.12 = (bf16[4,2,144,256]{3,2,1,0:T(8,128)(2,1)}, bf16[4,2,144,256]{3,2,1,0:T(8,128)(2,1)S(1)}, u32[]{:S(2)}, u32[]{:S(2)}) collective-permute-start(bf16[4,2,144,256]{3,2,1,0:T(8,128)(2,1)} %get-tuple-element.141), channel_id=1, source_target_pairs={{0,8},{8,0},{16,24},{24,16},{1,9},{9,1},{17,25},{25,17},{2,10},{10... | collective-permute-start | bytes 1769480 | tf_op jit(solution)/shard_map/ppermute | solution.py:896
  302.4 21.9 %collective-permute-start.36 = (bf16[4,2,128,256]{3,2,1,0:T(8,128)(2,1)}, bf16[4,2,128,256]{3,2,1,0:T(8,128)(2,1)S(1)}, u32[]{:S(2)}, u32[]{:S(2)}) collective-permute-start(bf16[4,2,128,256]{3,2,1,0:T(8,128)(2,1)} %get-tuple-element.173), channel_id=1, source_target_pairs={{0,8},{8,0},{16,24},{24,16},{1,9},{9,1},{17,25},{25,17},{2,10},{10... | collective-permute-start | bytes 1572872 | tf_op jit(solution)/shard_map/ppermute | solution.py:896
  303.9 21.8 %collective-permute-start.13 = (bf16[4,2,144,256]{3,2,1,0:T(8,128)(2,1)}, bf16[4,2,144,256]{3,2,1,0:T(8,128)(2,1)}, u32[]{:S(2)}, u32[]{:S(2)}) collective-permute-start(bf16[4,2,144,256]{3,2,1,0:T(8,128)(2,1)} %get-tuple-element.143), channel_id=1, source_target_pairs={{0,16},{8,24},{16,0},{24,8},{1,17},{9,25},{17,1},{25,9},{2,18},{10... | collective-permute-start | bytes 1769480 | tf_op jit(solution)/shard_map/ppermute | solution.py:897
  324.3 19.8 %collective-permute-start.48 = (bf16[4,512,256]{2,1,0:T(8,128)(2,1)}, bf16[4,512,256]{2,1,0:T(8,128)(2,1)S(1)}, u32[]{:S(2)}, u32[]{:S(2)}) collective-permute-start(bf16[4,512,256]{2,1,0:T(8,128)(2,1)} %get-tuple-element.189), channel_id=1, source_target_pairs={{0,1},{1,0},{2,3},{3,2},{4,5},{5,4},{6,7},{7,6},{8,9},{9,8},{10,11... | collective-permute-start | bytes 3145736 | tf_op jit(solution)/shard_map/ppermute | solution.py:881
  325.1 20.9 %collective-permute-start.24 = (bf16[4,512,256]{2,1,0:T(8,128)(2,1)}, bf16[4,512,256]{2,1,0:T(8,128)(2,1)S(1)}, u32[]{:S(2)}, u32[]{:S(2)}) collective-permute-start(bf16[4,512,256]{2,1,0:T(8,128)(2,1)} %get-tuple-element.157), channel_id=1, source_target_pairs={{0,1},{1,0},{2,3},{3,2},{4,5},{5,4},{6,7},{7,6},{8,9},{9,8},{10,11... | collective-permute-start | bytes 3145736 | tf_op jit(solution)/shard_map/ppermute | solution.py:881
  339.8 24.8 %collective-permute-start.14 = (bf16[4,144,256]{2,1,0:T(8,128)(2,1)}, bf16[4,144,256]{2,1,0:T(8,128)(2,1)S(1)}, u32[]{:S(2)}, u32[]{:S(2)}) collective-permute-start(bf16[4,144,256]{2,1,0:T(8,128)(2,1)} %get-tuple-element.145), channel_id=1, source_target_pairs={{0,16},{8,24},{16,0},{24,8},{1,17},{9,25},{17,1},{25,9},{2,18},{10... | collective-permute-start | bytes 884744 | tf_op jit(solution)/shard_map/ppermute | solution.py:908
  347.2 20.1 %collective-permute-start.15 = (bf16[4,144,256]{2,1,0:T(8,128)(2,1)}, bf16[4,144,256]{2,1,0:T(8,128)(2,1)}, u32[]{:S(2)}, u32[]{:S(2)}) collective-permute-start(bf16[4,144,256]{2,1,0:T(8,128)(2,1)} %get-tuple-element.147), channel_id=1, source_target_pairs={{0,8},{8,0},{16,24},{24,16},{1,9},{9,1},{17,25},{25,17},{2,10},{10... | collective-permute-start | bytes 884744 | tf_op jit(solution)/shard_map/ppermute | solution.py:909
  361.0 28.2 %collective-permute-start.49 = (bf16[4,2,240,256]{3,2,1,0:T(8,128)(2,1)}, bf16[4,2,240,256]{3,2,1,0:T(8,128)(2,1)S(1)}, u32[]{:S(2)}, u32[]{:S(2)}) collective-permute-start(bf16[4,2,240,256]{3,2,1,0:T(8,128)(2,1)} %get-tuple-element.191), channel_id=1, source_target_pairs={{0,8},{8,0},{16,24},{24,16},{1,9},{9,1},{17,25},{25,17},{2,10},{10... | collective-permute-start | bytes 2949128 | tf_op jit(solution)/shard_map/ppermute | solution.py:896
  361.6 31.5 %collective-permute-start.50 = (bf16[4,2,240,256]{3,2,1,0:T(8,128)(2,1)}, bf16[4,2,240,256]{3,2,1,0:T(8,128)(2,1)}, u32[]{:S(2)}, u32[]{:S(2)}) collective-permute-start(bf16[4,2,240,256]{3,2,1,0:T(8,128)(2,1)} %get-tuple-element.193), channel_id=1, source_target_pairs={{0,16},{8,24},{16,0},{24,8},{1,17},{9,25},{17,1},{25,9},{2,18},{10... | collective-permute-start | bytes 2949128 | tf_op jit(solution)/shard_map/ppermute | solution.py:897
  363.2 42.6 %collective-permute-start.25 = (bf16[4,2,240,256]{3,2,1,0:T(8,128)(2,1)}, bf16[4,2,240,256]{3,2,1,0:T(8,128)(2,1)}, u32[]{:S(2)}, u32[]{:S(2)}) collective-permute-start(bf16[4,2,240,256]{3,2,1,0:T(8,128)(2,1)} %get-tuple-element.159), channel_id=1, source_target_pairs={{0,8},{8,0},{16,24},{24,16},{1,9},{9,1},{17,25},{25,17},{2,10},{10... | collective-permute-start | bytes 2949128 | tf_op jit(solution)/shard_map/ppermute | solution.py:896
  364.7 42.6 %collective-permute-start.26 = (bf16[4,2,240,256]{3,2,1,0:T(8,128)(2,1)}, bf16[4,2,240,256]{3,2,1,0:T(8,128)(2,1)}, u32[]{:S(2)}, u32[]{:S(2)}) collective-permute-start(bf16[4,2,240,256]{3,2,1,0:T(8,128)(2,1)} %get-tuple-element.161), channel_id=1, source_target_pairs={{0,16},{8,24},{16,0},{24,8},{1,17},{9,25},{17,1},{25,9},{2,18},{10... | collective-permute-start | bytes 2949128 | tf_op jit(solution)/shard_map/ppermute | solution.py:897
  385.7 22.1 %collective-permute-start.16 = (bf16[2,144,256]{2,1,0:T(8,128)(2,1)}, bf16[2,144,256]{2,1,0:T(8,128)(2,1)S(1)}, u32[]{:S(2)}, u32[]{:S(2)}) collective-permute-start(bf16[2,144,256]{2,1,0:T(8,128)(2,1)} %get-tuple-element.149), channel_id=1, source_target_pairs={{0,2},{1,3},{2,4},{3,5},{4,6},{5,7},{6,0},{7,1},{8,10},{9,11},{10,... | collective-permute-start | bytes 442376 | tf_op jit(solution)/shard_map/ppermute | solution.py:921
  389.3 29.6 %collective-permute-start.17 = (bf16[2,144,256]{2,1,0:T(8,128)(2,1)}, bf16[2,144,256]{2,1,0:T(8,128)(2,1)S(1)}, u32[]{:S(2)}, u32[]{:S(2)}) collective-permute-start(bf16[2,144,256]{2,1,0:T(8,128)(2,1)} %get-tuple-element.150), channel_id=1, source_target_pairs={{0,4},{1,5},{2,6},{3,7},{4,0},{5,1},{6,2},{7,3},{8,12},{9,13},{10,... | collective-permute-start | bytes 442376 | tf_op jit(solution)/shard_map/ppermute | solution.py:921
  393.1 27.3 %collective-permute-start.18 = (bf16[2,144,256]{2,1,0:T(8,128)(2,1)}, bf16[2,144,256]{2,1,0:T(8,128)(2,1)S(1)}, u32[]{:S(2)}, u32[]{:S(2)}) collective-permute-start(bf16[2,144,256]{2,1,0:T(8,128)(2,1)} %get-tuple-element.151), channel_id=1, source_target_pairs={{0,6},{1,7},{2,0},{3,1},{4,2},{5,3},{6,4},{7,5},{8,14},{9,15},{10,... | collective-permute-start | bytes 442376 | tf_op jit(solution)/shard_map/ppermute | solution.py:921
  405.8 17.2 %collective-permute-start.45 = (bf16[2,128,256]{2,1,0:T(8,128)(2,1)}, bf16[2,128,256]{2,1,0:T(8,128)(2,1)S(1)}, u32[]{:S(2)}, u32[]{:S(2)}) collective-permute-start(bf16[2,128,256]{2,1,0:T(8,128)(2,1)} %sum_four.6), channel_id=1, source_target_pairs={{0,24},{8,16},{16,8},{24,0},{1,25},{9,17},{17,9},{25,1},{2,26},{10... | collective-permute-start | bytes 393224 | tf_op jit(solution)/shard_map/ppermute | solution.py:932
  407.8 18.0 %collective-permute-start.43 = (bf16[2,128,256]{2,1,0:T(8,128)(2,1)}, bf16[2,128,256]{2,1,0:T(8,128)(2,1)S(1)}, u32[]{:S(2)}, u32[]{:S(2)}) collective-permute-start(bf16[2,128,256]{2,1,0:T(8,128)(2,1)} %sum_four.6), channel_id=1, source_target_pairs={{0,8},{8,0},{16,24},{24,16},{1,9},{9,1},{17,25},{25,17},{2,10},{10... | collective-permute-start | bytes 393224 | tf_op jit(solution)/shard_map/ppermute | solution.py:932
  418.8 33.5 %collective-permute-start.51 = (bf16[4,240,256]{2,1,0:T(8,128)(2,1)}, bf16[4,240,256]{2,1,0:T(8,128)(2,1)S(1)}, u32[]{:S(2)}, u32[]{:S(2)}) collective-permute-start(bf16[4,240,256]{2,1,0:T(8,128)(2,1)} %get-tuple-element.195), channel_id=1, source_target_pairs={{0,16},{8,24},{16,0},{24,8},{1,17},{9,25},{17,1},{25,9},{2,18},{10... | collective-permute-start | bytes 1474568 | tf_op jit(solution)/shard_map/ppermute | solution.py:908
  420.4 31.9 %collective-permute-start.52 = (bf16[4,240,256]{2,1,0:T(8,128)(2,1)}, bf16[4,240,256]{2,1,0:T(8,128)(2,1)S(1)}, u32[]{:S(2)}, u32[]{:S(2)}) collective-permute-start(bf16[4,240,256]{2,1,0:T(8,128)(2,1)} %get-tuple-element.197), channel_id=1, source_target_pairs={{0,8},{8,0},{16,24},{24,16},{1,9},{9,1},{17,25},{25,17},{2,10},{10... | collective-permute-start | bytes 1474568 | tf_op jit(solution)/shard_map/ppermute | solution.py:909
  423.0 37.5 %collective-permute-start.27 = (bf16[4,240,256]{2,1,0:T(8,128)(2,1)}, bf16[4,240,256]{2,1,0:T(8,128)(2,1)S(1)}, u32[]{:S(2)}, u32[]{:S(2)}) collective-permute-start(bf16[4,240,256]{2,1,0:T(8,128)(2,1)} %get-tuple-element.163), channel_id=1, source_target_pairs={{0,16},{8,24},{16,0},{24,8},{1,17},{9,25},{17,1},{25,9},{2,18},{10... | collective-permute-start | bytes 1474568 | tf_op jit(solution)/shard_map/ppermute | solution.py:908
  425.8 21.2 %collective-permute-start.20 = (bf16[2,144,256]{2,1,0:T(8,128)(2,1)}, bf16[2,144,256]{2,1,0:T(8,128)(2,1)S(1)}, u32[]{:S(2)}, u32[]{:S(2)}) collective-permute-start(bf16[2,144,256]{2,1,0:T(8,128)(2,1)} %sum_four.4), channel_id=1, source_target_pairs={{0,16},{8,24},{16,0},{24,8},{1,17},{9,25},{17,1},{25,9},{2,18},{10... | collective-permute-start | bytes 442376 | tf_op jit(solution)/shard_map/ppermute | solution.py:932
  434.6 25.9 %collective-permute-start.28 = (bf16[4,240,256]{2,1,0:T(8,128)(2,1)}, bf16[4,240,256]{2,1,0:T(8,128)(2,1)S(1)}, u32[]{:S(2)}, u32[]{:S(2)}) collective-permute-start(bf16[4,240,256]{2,1,0:T(8,128)(2,1)} %get-tuple-element.165), channel_id=1, source_target_pairs={{0,8},{8,0},{16,24},{24,16},{1,9},{9,1},{17,25},{25,17},{2,10},{10... | collective-permute-start | bytes 1474568 | tf_op jit(solution)/shard_map/ppermute | solution.py:909
  457.4 30.5 %collective-permute-start.54 = (bf16[2,240,256]{2,1,0:T(8,128)(2,1)}, bf16[2,240,256]{2,1,0:T(8,128)(2,1)S(1)}, u32[]{:S(2)}, u32[]{:S(2)}) collective-permute-start(bf16[2,240,256]{2,1,0:T(8,128)(2,1)} %get-tuple-element.200), channel_id=1, source_target_pairs={{0,4},{1,5},{2,6},{3,7},{4,0},{5,1},{6,2},{7,3},{8,12},{9,13},{10,... | collective-permute-start | bytes 737288 | tf_op jit(solution)/shard_map/ppermute | solution.py:921
  458.8 29.2 %collective-permute-start.55 = (bf16[2,240,256]{2,1,0:T(8,128)(2,1)}, bf16[2,240,256]{2,1,0:T(8,128)(2,1)S(1)}, u32[]{:S(2)}, u32[]{:S(2)}) collective-permute-start(bf16[2,240,256]{2,1,0:T(8,128)(2,1)} %get-tuple-element.201), channel_id=1, source_target_pairs={{0,6},{1,7},{2,0},{3,1},{4,2},{5,3},{6,4},{7,5},{8,14},{9,15},{10,... | collective-permute-start | bytes 737288 | tf_op jit(solution)/shard_map/ppermute | solution.py:921
  464.0 29.2 %collective-permute-start.29 = (bf16[2,240,256]{2,1,0:T(8,128)(2,1)}, bf16[2,240,256]{2,1,0:T(8,128)(2,1)S(1)}, u32[]{:S(2)}, u32[]{:S(2)}) collective-permute-start(bf16[2,240,256]{2,1,0:T(8,128)(2,1)} %get-tuple-element.167), channel_id=1, source_target_pairs={{0,2},{1,3},{2,4},{3,5},{4,6},{5,7},{6,0},{7,1},{8,10},{9,11},{10,... | collective-permute-start | bytes 737288 | tf_op jit(solution)/shard_map/ppermute | solution.py:921
  464.5 31.8 %collective-permute-start.30 = (bf16[2,240,256]{2,1,0:T(8,128)(2,1)}, bf16[2,240,256]{2,1,0:T(8,128)(2,1)S(1)}, u32[]{:S(2)}, u32[]{:S(2)}) collective-permute-start(bf16[2,240,256]{2,1,0:T(8,128)(2,1)} %get-tuple-element.168), channel_id=1, source_target_pairs={{0,4},{1,5},{2,6},{3,7},{4,0},{5,1},{6,2},{7,3},{8,12},{9,13},{10,... | collective-permute-start | bytes 737288 | tf_op jit(solution)/shard_map/ppermute | solution.py:921
  469.5 28.3 %collective-permute-start.31 = (bf16[2,240,256]{2,1,0:T(8,128)(2,1)}, bf16[2,240,256]{2,1,0:T(8,128)(2,1)S(1)}, u32[]{:S(2)}, u32[]{:S(2)}) collective-permute-start(bf16[2,240,256]{2,1,0:T(8,128)(2,1)} %get-tuple-element.169), channel_id=1, source_target_pairs={{0,6},{1,7},{2,0},{3,1},{4,2},{5,3},{6,4},{7,5},{8,14},{9,15},{10,... | collective-permute-start | bytes 737288 | tf_op jit(solution)/shard_map/ppermute | solution.py:921
  (65 other events, 607.3 us)
